TPU v7x, 256 devices: a whole 4x4x8 slice. The times are simulated.
256 devices in a mesh: pool: 2 (over core), rep: 8 (over y_hi, x), tp: 16 (over z, y_lo).
Axes of the slice: x: 4, y: 4 (y_hi: 2, y_lo: 2; y = y_hi * 2 + y_lo), z: 8, core: 2. Of those that a mesh axis runs over, the one named last changes fastest.
Arguments:
- prompt_states: bfloat16 [2, 8, 1024, 8192], P('pool', 'rep', 'tp'), may hold values from -6 to 6
- w_query: bfloat16 [8192, 8192], P(None, 'tp'), may hold values from -9 to 9
- w_kv: bfloat16 [8192, 2048], P(None, 'tp'), may hold values from -0.0625 to 0.0625
- queries: bfloat16 [2, 8, 4, 64, 8192], P('pool', 'rep', None, None, 'tp'), may hold values from -110 to 110
- new_kv: bfloat16 [2, 8, 4, 64, 2048], P('pool', 'rep', None, None, 'tp'), may hold values from -6 to 6
- lengths: int32 [2, 8, 4], replicated, may hold values from 1 to 512, 1024 in all within a row
- pairing: int32 [2, 8], replicated, may hold values from 0 to 7, as said below
- assign: int32 [2, 8, 64], P('pool', 'rep'), may hold values from 0 to 3
- cache_len: int32 [2, 8, 64], P('pool', 'rep'), may hold values from 1 to 512
Outputs:
- prefill_out: bfloat16 [2, 8, 1024, 8192], P('pool', 'rep', None, 'tp')
- decode_out: bfloat16 [2, 8, 4, 64, 8192], P('pool', 'rep', None, None, 'tp')
Inputs may be any that keep to these rules, and one draw needn't show every extreme that they name: Each pool's row of pairing is a permutation of 0 to 7 with pairing[p, 0] = 7 and pairing[p, d] = d for some d.
All inputs are finite; a program needn't handle non-finite values.
Results may differ from a plain program's by a relative error of at most 0.012.
The roundings to bfloat16 on the way count: a program that leaves them out, or rounds other values in their place, can miss the bound.
Values may be sent and summed in bfloat16 or wider, within the bound.
A program may use at most 128 MiB of HBM per device.

v0:
```python
import math

import jax
import jax.numpy as jnp
from jax import lax
from jax.sharding import PartitionSpec as P

HD = 128


theta_base = 500000.0
neg_large = -1e30


def from_partner(block, axis, stride):
    count = lax.axis_size(axis)
    route = []
    for low in range(count):
        high = low | 1 << stride
        if high != low and high < count:
            route += [(low, high), (high, low)]
    return lax.ppermute(block, axis, route)


def rotate(vectors, positions):
    half_dim = vectors.shape[-1] // 2
    inverse = theta_base ** (-(jnp.arange(half_dim, dtype=jnp.float32) / half_dim))
    angles = positions[:, None] * inverse[None, :]
    target = (positions.shape[0],) + (1,) * (vectors.ndim - 2) + (half_dim,)
    cosine = jnp.cos(angles).reshape(target)
    sine_term = jnp.sin(angles).reshape(target)
    former = vectors[..., :half_dim]
    latter = vectors[..., half_dim:]
    return jnp.concatenate(
        [former * cosine - latter * sine_term, latter * cosine + former * sine_term], axis=-1
    )


def token_layout(lengths, token_count):
    span_ends = jnp.cumsum(lengths)
    starts = span_ends - lengths
    token_index = jnp.arange(token_count, dtype=jnp.int32)
    segment = jnp.sum((token_index[:, None] >= span_ends[None, :]).astype(jnp.int32), axis=1)
    member = segment[:, None] == jnp.arange(lengths.shape[0], dtype=jnp.int32)[None, :]
    anchor = jnp.sum(jnp.where(member, starts[None, :], 0), axis=1)
    return (segment, (token_index - anchor).astype(jnp.float32))


def decode_mask(lengths, row_assign, row_len, spots):
    starts = jnp.cumsum(lengths) - lengths
    member = row_assign[:, None] == jnp.arange(lengths.shape[0], dtype=jnp.int32)[None, :]
    lower = jnp.sum(jnp.where(member, starts[None, :], 0), axis=1)
    extent = jnp.sum(jnp.where(member, lengths[None, :], 0), axis=1)
    upper = lower + jnp.minimum(extent, row_len)
    return (spots[None, :] >= lower[:, None]) & (spots[None, :] < upper[:, None])


def select_row(table, first_index, second_index):
    member = (jnp.arange(table.shape[0], dtype=jnp.int32)[:, None] == first_index) & (
        jnp.arange(table.shape[1], dtype=jnp.int32)[None, :] == second_index
    )
    return jnp.sum(jnp.where(member[:, :, None], table, 0), axis=(0, 1))


def prefill_attend(query, key_rows, value_rows, segment):
    token_count = query.shape[0]
    inv_root = 1.0 / math.sqrt(query.shape[-1])
    scores = (
        jnp.einsum("qkgd,tkd->kgqt", query, key_rows, preferred_element_type=jnp.float32) * inv_root
    )
    token_index = jnp.arange(token_count, dtype=jnp.int32)
    allowed = (segment[:, None] == segment[None, :]) & (
        token_index[None, :] <= token_index[:, None]
    )
    scores = jnp.where(allowed, scores, neg_large)
    peak = jnp.max(scores, axis=-1, keepdims=True)
    weights = jnp.where(allowed, jnp.exp(scores - peak), 0.0)
    rounded = (weights / jnp.sum(weights, axis=-1, keepdims=True)).astype(jnp.bfloat16)
    mixed = jnp.einsum("kgqt,tkd->qkgd", rounded, value_rows, preferred_element_type=jnp.float32)
    return mixed.astype(jnp.bfloat16).reshape(token_count, -1)


def cache_partial(query, key_rows, value_rows, visible):
    inv_root = 1.0 / math.sqrt(query.shape[-1])
    scores = (
        jnp.einsum("srkgd,pkd->srkgp", query, key_rows, preferred_element_type=jnp.float32)
        * inv_root
    )
    allowed = visible[None, :, None, None, :]
    scores = jnp.where(allowed, scores, neg_large)
    peak = jnp.max(scores, axis=-1)
    weights = jnp.where(allowed, jnp.exp(scores - peak[..., None]), 0.0)
    total = jnp.sum(weights, axis=-1)
    mixed = jnp.einsum("srkgp,pkd->srkgd", weights, value_rows.astype(jnp.float32))
    steps_count, row_count, kv_count, group_size = peak.shape
    heads_all = kv_count * group_size
    return (
        peak.reshape(1, steps_count, row_count, heads_all),
        total.reshape(1, steps_count, row_count, heads_all),
        mixed.reshape(1, steps_count, row_count, heads_all, query.shape[-1]),
    )


def finish(peaks, totals, mixes, query, fresh):
    steps_count, row_count, kv_count, group_size, head_size = query.shape
    heads_here = kv_count * group_size
    inv_root = 1.0 / math.sqrt(head_size)
    own_scores = (
        jnp.einsum(
            "srkgd,urkd->srkgu", query, fresh[:, :, :, 0], preferred_element_type=jnp.float32
        )
        * inv_root
    )
    step_index = jnp.arange(steps_count, dtype=jnp.int32)
    own_valid = (step_index[:, None] >= step_index[None, :])[:, None, None, None, :]
    own_scores = jnp.where(own_valid, own_scores, neg_large)
    own_peak = jnp.max(own_scores, axis=-1).reshape(steps_count, row_count, heads_here)
    peak = jnp.maximum(jnp.max(peaks, axis=0), own_peak)
    factors = jnp.exp(peaks - peak[None])
    own_weights = jnp.where(
        own_valid,
        jnp.exp(own_scores - peak.reshape(steps_count, row_count, kv_count, group_size)[..., None]),
        0.0,
    )
    total = jnp.sum(totals * factors, axis=0) + jnp.sum(own_weights, axis=-1).reshape(
        steps_count, row_count, heads_here
    )
    own_mix = jnp.einsum(
        "srkgu,urkd->srkgd", own_weights, fresh[:, :, :, 1].astype(jnp.float32)
    ).reshape(steps_count, row_count, heads_here, head_size)
    mixed = jnp.sum(mixes * factors[..., None], axis=0) + own_mix
    return (
        (mixed / total[..., None])
        .astype(jnp.bfloat16)
        .reshape(steps_count, row_count, heads_here * head_size)
    )


def hand_over(cache_piece, wanted):
    shard_rows = lax.all_gather(cache_piece[None], ("pool", "rep"), axis=0, tiled=True)
    shard_count = shard_rows.shape[0]
    member = jnp.arange(shard_count, dtype=jnp.int32) == wanted
    member = member.reshape((shard_count,) + (1,) * (shard_rows.ndim - 1))
    return jnp.sum(jnp.where(member, shard_rows, jnp.zeros_like(shard_rows)), axis=0)


def per_device(prompt_states, w_query, w_kv, queries, new_kv, lengths, pairing, assign, cache_len):
    tp_index = lax.axis_index("tp")
    pool_index = lax.axis_index("pool")
    rep_index = lax.axis_index("rep")
    rep_count = lax.axis_size("rep")
    local_rows = prompt_states.reshape(-1, prompt_states.shape[-1])
    query_cols = w_query.shape[1]
    kv_cols = w_kv.shape[1]
    shard_rows = lax.all_gather(local_rows, "tp", axis=0, tiled=True)
    projected = jnp.concatenate(
        [
            jnp.dot(shard_rows, w_query, preferred_element_type=jnp.float32),
            jnp.dot(shard_rows, w_kv, preferred_element_type=jnp.float32),
        ],
        axis=1,
    )
    token_count = projected.shape[0]
    heads_here = query_cols // HD
    own_lengths = select_row(lengths, pool_index, rep_index)
    segment, positions = token_layout(own_lengths, token_count)
    query = rotate(
        projected[:, :query_cols].reshape(token_count, heads_here, HD), positions
    ).astype(jnp.bfloat16)
    steps_count = queries.shape[2]
    row_count = queries.shape[3]
    new_local = new_kv.reshape(steps_count, row_count, kv_cols)
    kv_count = 1
    raw_cols = projected[:, query_cols:]
    is_even = tp_index % 2 == 0
    own_half = jnp.where(is_even, rotate(raw_cols[:, None, :], positions)[:, 0], raw_cols).astype(
        jnp.bfloat16
    )
    other_half, new_other = from_partner((own_half, new_local), "tp", 0)
    key_rows = jnp.where(is_even, own_half, other_half)[:, None, :]
    value_rows = jnp.where(is_even, other_half, own_half)[:, None, :]
    cache_local = jnp.stack([key_rows, value_rows], axis=2)
    fresh = jnp.stack(
        [jnp.where(is_even, new_local, new_other), jnp.where(is_even, new_other, new_local)], axis=2
    )[:, :, None]
    group_size = heads_here // kv_count
    attended = prefill_attend(
        query.reshape(token_count, kv_count, group_size, HD), key_rows, value_rows, segment
    )
    prefill_out = attended.reshape(1, 1, token_count, query_cols)
    paired = select_row(pairing[:, :, None], pool_index, rep_index)[0]
    other_pool = (pool_index + 1) % 2
    wanted = other_pool * rep_count + paired
    pair_lengths = select_row(lengths, other_pool, paired)
    row_assign = assign.reshape(row_count)
    row_len = cache_len.reshape(row_count)
    local_query = queries.reshape(steps_count, row_count, kv_count, group_size, HD)
    received = hand_over(cache_local, wanted)
    visible = decode_mask(
        pair_lengths, row_assign, row_len, jnp.arange(token_count, dtype=jnp.int32)
    )
    peaks, totals, mixes = cache_partial(local_query, received[:, :, 0], received[:, :, 1], visible)
    decoded = finish(peaks, totals, mixes, local_query, fresh)
    return (prefill_out, decoded.reshape(1, 1, steps_count, row_count, query_cols))


def solution(mesh):
    placed = (
        P("pool", "rep", "tp", None),
        P(None, "tp"),
        P(None, "tp"),
        P("pool", "rep", None, None, "tp"),
        P("pool", "rep", None, None, "tp"),
        P(),
        P(),
        P("pool", "rep", None),
        P("pool", "rep", None),
    )
    return jax.shard_map(
        per_device,
        mesh=mesh,
        in_specs=placed,
        out_specs=(P("pool", "rep", None, "tp"), P("pool", "rep", None, None, "tp")),
        check_vma=False,
    )
```

profile of v0, /device:TPU:1, one launch (start us, length us, event | category | flops | bytes accessed | tf_op | source)
XLA Modules:
  0.0 509.5 jit_solution(11620626266200361069)
XLA Ops:
  7.2 0.7 all-gather.5.cloned.1.call-update
  8.0 1.4 select_reduce_fusion.6
  9.4 0.6 iota_compare_fusion.7
  10.1 0.8 select_reduce_fusion.2
  11.4 353.3 %all-gather.5.cloned.1.call-done = bf16[1,1,1024,8192]{3,2,1,0:T(8,128)(2,1)} async-done(((bf16[1,1,64,8192]{3,2,1,0:T(8,128)(2,1)}), bf16[1,1,1024,8192]{3,2,1,0:T(8,128)(2,1)}) %all-gather.5.cloned.1.call-update) | async-done | bytes 16777232 | tf_op jit(solution)/shard_map/all_gather | solution.py:155
  364.6 11.4 %fusion.2 = f32[1024,128]{0,1:T(8,128)S(1)} fusion(bf16[8192,128]{1,0:T(8,128)(2,1)S(1)} %copy-done, bf16[1,1,1024,8192]{3,2,1,0:T(8,128)(2,1)} %all-gather.5.cloned.1.call-done), kind=kOutput, calls=%fused_computation.3 | convolution fusion | flops 2147483648 | bytes 19398656 | tf_op jit(solution)/shard_map/dot_general | solution.py:159
  376.1 1.2 fusion.39
  377.5 7.2 %collective-permute-done = bf16[1024,128]{0,1:T(8,128)(2,1)S(1)} collective-permute-done((bf16[1024,128]{0,1:T(8,128)(2,1)S(1)}, bf16[1024,128]{0,1:T(8,128)(2,1)S(1)}, u32[]{:S(2)}, u32[]{:S(2)}) %collective-permute-start) | collective-permute-done | bytes 262176 | tf_op jit(solution)/shard_map/ppermute | solution.py:22
  384.7 0.9 pad_maximum_fusion
  385.6 0.6 collective-permute-start.1
  387.4 3.1 multiply_cosine_fusion
  390.5 0.6 fusion.10
  391.3 3.3 fusion.62
  394.8 17.3 %fusion = f32[1024,512]{0,1:T(8,128)S(1)} fusion(bf16[8192,512]{1,0:T(8,128)(2,1)} %param.10, bf16[1,1,1024,8192]{3,2,1,0:T(8,128)(2,1)} %all-gather.5.cloned.1.call-done), kind=kOutput, calls=%fused_computation.1 | convolution fusion | flops 8589934592 | bytes 27262976 | tf_op jit(solution)/shard_map/dot_general | solution.py:158
  412.0 1.6 fusion.61
  413.6 1.8 copy.101
  415.4 3.2 copy.100
  418.6 2.4 subtract_convert_fusion
  421.1 3.9 fusion.4
  425.0 4.2 fusion.5
  429.2 6.1 %fusion.18 = bf16[128,4,1024]{2,0,1:T(8,128)(2,1)S(1)} fusion(f32[4,1024]{1,0:T(4,128)S(1)} %fusion.5, f32[4,1024]{1,0:T(4,128)S(1)} %get-tuple-element.32, f32[1024,1024,4]{1,0,2:T(8,128)S(1)} %get-tuple-element.33, pred[1024,1024]{0,1:T(8,128)(4,1)S(1)} %fusion.10, bf16[1024,128]{0,1:T(8,128)(2,1)S(1)} %copy-done.9, bf16[1024,128]{0,1:T(8,128)(2,1)S(1)} %copy-done.4, ...), kind=kOutput, calls=%fused_computation.27 | convolution fusion | flops 1099563008 | bytes 19431424 | tf_op jit(solution)/shard_map/kgqt,tkd->qkgd/dot_general | solution.py:79
  435.3 1.5 copy.89
  436.7 33.3 %all-gather.7.cloned.1.call-done = bf16[16384,1,2,128]{0,3,2,1:T(8,128)(2,1)} async-done(((bf16[1024,1,2,128]{0,3,2,1:T(8,128)(2,1)}), bf16[16384,1,2,128]{0,3,2,1:T(8,128)(2,1)}) %all-gather.7.cloned.1.call-update) | async-done | bytes 8388624 | tf_op jit(solution)/shard_map/all_gather | solution.py:140
  470.1 15.2 %copy.102 = bf16[32,8,16,1024]{3,2,1,0:T(8,128)(2,1)} copy(bf16[32,8,16,1024]{3,1,2,0:T(8,128)(2,1)} %bitcast.168) | data formatting | bytes 16777216
  485.2 6.1 %select_reduce_fusion = bf16[1024,2,128]{0,2,1:T(8,128)(2,1)S(1)} fusion(bf16[16,1024,1,2,128]{1,0,4,3,2:T(8,128)(2,1)} %bitcast.167, pred[16]{0:T(512)(128)(4,1)S(1)} %iota_compare_fusion.9), kind=kLoop, calls=%fused_computation.11 | loop fusion | flops 8126464 | bytes 8912912 | tf_op jit(solution)/shard_map/reduce_sum | solution.py:144
  491.8 0.9 fusion.11
  492.7 1.2 fusion.21
  493.9 1.3 fusion.12
  496.0 2.2 convolution_bitcast_fusion
  498.6 1.1 copy.99
  500.7 1.0 fusion.33
  501.7 0.7 copy.90
  (64 shorter events, 4.1 us)
Async XLA Ops:
  7.2 357.5 %copy-start = (bf16[8192,128]{1,0:T(8,128)(2,1)S(1)}, bf16[8192,128]{1,0:T(8,128)(2,1)}, u32[]{:S(2)}) copy-start(bf16[8192,128]{1,0:T(8,128)(2,1)} %param.11) | copy-start | bytes 6291460
  7.2 357.4 %all-gather.5.cloned.1.call-start = ((), (), s32[]{:S(2)}) async-start(), calls=%async_computation | async-start | bytes 17825792 | tf_op jit(solution)/shard_map/all_gather | solution.py:155
  7.9 462.1 %all-gather.7.cloned.1.call-start = ((), (), s32[]{:S(2)}) async-start(), calls=%async_computation.1 | async-start | bytes 8912896 | tf_op jit(solution)/shard_map/all_gather | solution.py:140
  376.1 9.5 %copy-start.7 = (bf16[1,1,4,64,128]{4,3,2,1,0:T(8,128)(2,1)S(1)}, bf16[1,1,4,64,128]{4,3,2,1,0:T(8,128)(2,1)}, u32[]{:S(2)}) copy-start(bf16[1,1,4,64,128]{4,3,2,1,0:T(8,128)(2,1)} %param.13) | copy-start | bytes 196612
  376.1 11.0 %copy-start.6 = (bf16[1,1,4,64,512]{4,3,2,1,0:T(8,128)(2,1)S(1)}, bf16[1,1,4,64,512]{4,3,2,1,0:T(8,128)(2,1)}, u32[]{:S(2)}) copy-start(bf16[1,1,4,64,512]{4,3,2,1,0:T(8,128)(2,1)} %param.12) | copy-start | bytes 786436
  376.1 11.1 %copy-start.10 = (s32[1,1,64]{2,1,0:T(1,128)S(1)}, s32[1,1,64]{2,1,0:T(1,128)}, u32[]{:S(2)}) copy-start(s32[1,1,64]{2,1,0:T(1,128)} %param.16) | copy-start | bytes 772
  376.1 11.1 %copy-start.11 = (s32[1,1,64]{2,1,0:T(1,128)S(1)}, s32[1,1,64]{2,1,0:T(1,128)}, u32[]{:S(2)}) copy-start(s32[1,1,64]{2,1,0:T(1,128)} %param.17) | copy-start | bytes 772
  377.3 17.3 %copy-start.3 = (bf16[1024,128]{0,1:T(8,128)(2,1)}, bf16[1024,128]{0,1:T(8,128)(2,1)S(1)}, u32[]{:S(2)}) copy-start(bf16[1024,128]{0,1:T(8,128)(2,1)S(1)} %fusion.31) | copy-start | bytes 786436
  377.4 7.3 %collective-permute-start = (bf16[1024,128]{0,1:T(8,128)(2,1)S(1)}, bf16[1024,128]{0,1:T(8,128)(2,1)S(1)}, u32[]{:S(2)}, u32[]{:S(2)}) collective-permute-start(bf16[1024,128]{0,1:T(8,128)(2,1)S(1)} %fusion.31), channel_id=1, source_target_pairs={{0,1},{1,0},{2,3},{3,2},{4,5},{5,4},{6,7},{7,6},{8,9},{9,8},{10,11... | collective-permute-start | bytes 786440 | tf_op jit(solution)/shard_map/ppermute | solution.py:22
  384.6 10.0 %copy-start.8 = (bf16[1024,128]{0,1:T(8,128)(2,1)}, bf16[1024,128]{0,1:T(8,128)(2,1)S(1)}, u32[]{:S(2)}) copy-start(bf16[1024,128]{0,1:T(8,128)(2,1)S(1)} %collective-permute-done) | copy-start | bytes 786436
  385.6 5.4 %collective-permute-start.1 = (bf16[4,64,128]{2,0,1:T(4,128)(2,1)S(1)}, bf16[4,64,128]{2,0,1:T(4,128)(2,1)S(1)}, u32[]{:S(2)}, u32[]{:S(2)}) collective-permute-start(bf16[4,64,128]{2,0,1:T(4,128)(2,1)S(1)} %bitcast.180), channel_id=1, source_target_pairs={{0,1},{1,0},{2,3},{3,2},{4,5},{5,4},{6,7},{7,6},{8,9},{9,8},{10,11... | collective-permute-start | bytes 196616 | tf_op jit(solution)/shard_map/ppermute | solution.py:22
  391.3 3.4 copy-start.5
  418.6 2.4 copy-start.4
  418.6 2.5 copy-start.9
  493.9 1.5 copy-start.2
  495.4 7.1 %copy-start.1 = (bf16[8192,128]{1,0:T(8,128)(2,1)S(1)}, bf16[8192,128]{1,0:T(8,128)(2,1)}, u32[]{:S(2)}) copy-start(bf16[8192,128]{1,0:T(8,128)(2,1)} %param.11) | copy-start | bytes 6291460
Sparse Core Ops, SparseCore 0:
  9.8 354.7 all-gather.4
  385.7 84.3 all-gather.6
where the time goes:
time: 515 us; the launch traced here: 510 us
  waiting for transfers between devices  394 us (77%)
  matrix products  46.2 us (9%)
  local copies, waits for them, and re-layouts  27.4 us (5%)
  other arithmetic  25.4 us (5%)
  between operations  15.4 us (3%)
    all_gather x1, waiting for transfers between devices, per_device(): shard_rows = lax.all_gather(local_rows, 'tp', axis=0, tiled=True)  353 us
    all_gather x1, waiting for transfers between devices, hand_over(): lax.all_gather(cache_piece[None], ('pool', 'rep'), axis=0, tiled=True)  33.3 us
    unnamed x30, local copies, waits for them, and re-layouts  22.5 us
    dot_general x1, matrix products, per_device(): jnp.dot(shard_rows, w_query, preferred_element_type=jnp.float32)  17.3 us
    dot_general x1, matrix products, per_device(): jnp.dot(shard_rows, w_kv, preferred_element_type=jnp.float32)  11.4 us
  transfers between devices with their start and end apart: 4, of which 3 were waited for; matrix products, arithmetic and copies ran while one was open for 10% of the time, Pallas kernels for 0%

commit v1 on v0

v1 whole, which is shorter than its diff:
```python
import functools
import math

import jax
import jax.numpy as jnp
import numpy as np
from jax import lax
from jax.experimental import pallas as pl
from jax.experimental.pallas import tpu as pltpu
from jax.sharding import PartitionSpec as P

HD = 128
PLANES = 8
REPS = 8
HEADS = 4
TOK = 64
HALF = 32
PLANE_ROWS = 2 * TOK
WINDOW = 5
STEPS = 4
ROWS = 64
NEW = STEPS * ROWS
CACHE = PLANES * PLANE_ROWS
W_LOW = 2560
K_CHUNK = 2048

theta_base = 500000.0
neg_large = -1e30
exp_scale = math.log2(math.e) / math.sqrt(HD)


def remote(src, dst, send_sem, recv_sem, device):
    pltpu.make_async_remote_copy(
        src_ref=src,
        dst_ref=dst,
        send_sem=send_sem,
        recv_sem=recv_sem,
        device_id=device,
        device_id_type=pl.DeviceIdType.MESH,
    ).start()


def landed(ref, sem):
    pltpu.make_async_copy(ref, ref, sem).wait()


def softmax_mix(scores, values):
    peak = jnp.max(scores, axis=-1, keepdims=True)
    weights = jnp.exp2((scores - peak) * exp_scale)
    total = jnp.sum(weights, axis=-1, keepdims=True)
    mixed = jnp.dot(weights.astype(jnp.bfloat16), values, preferred_element_type=jnp.float32)
    return mixed / total


def scores_of(query, keys):
    return lax.dot_general(
        query, keys, (((1,), (1,)), ((), ())), preferred_element_type=jnp.float32
    )


def kernel(
    x_hbm,
    wq_hbm,
    wkv_hbm,
    queries_ref,
    new_ref,
    lengths_ref,
    pairing_ref,
    assign_ref,
    cache_len_ref,
    freq_ref,
    prefill_ref,
    decode_ref,
    xg,
    wq,
    wkv,
    acc,
    cos_t,
    sin_t,
    bias,
    qhome,
    qstage,
    kvhome,
    kvstage,
    p1,
    p2,
    dec,
    x0_sem,
    xs_send,
    w_sem,
    w_send,
    up_send,
    up_recv,
    down_send,
    down_recv,
    sib_send,
    sib_recv,
    new_send,
    new_recv,
    q_send,
    q_recv,
    kv_send,
    kv_send2,
    kv_recv,
    p1_send,
    p1_recv,
    p2_send,
    p2_recv,
):
    core = lax.axis_index("pool")
    rep = lax.axis_index("rep")
    t = lax.axis_index("tp")
    z = t // 2
    y = t % 2
    diag = core == y
    off = core != y
    other = 1 - core

    def dev(c2, g2, z2, y2):
        return (c2, g2, z2 * 2 + y2)

    up_dev = dev(core, rep, (z + 1) % PLANES, y)
    down_dev = dev(core, rep, (z + PLANES - 1) % PLANES, y)
    sibling = dev(other, rep, z, y)
    swap_low = dev(other, rep, z, 1 - y)
    swap_high = dev(other, (rep + REPS // 2) % REPS, z, 1 - y)
    across = dev(core, rep, z, 1 - y)
    row0 = pl.multiple_of(core * TOK, TOK)
    other_row0 = pl.multiple_of(other * TOK, TOK)

    wq_low = wq.at[pl.ds(0, W_LOW)]
    wq_high = wq.at[pl.ds(W_LOW, wq.shape[0] - W_LOW)]
    wq_hbm_low = wq_hbm.at[pl.ds(0, W_LOW)]
    wq_hbm_high = wq_hbm.at[pl.ds(W_LOW, wq.shape[0] - W_LOW)]

    def block(slot, half):
        return xg.at[slot, pl.ds(pl.multiple_of(row0 + half * HALF, HALF), HALF)]

    def sibling_block(slot, half):
        return xg.at[slot, pl.ds(pl.multiple_of(other_row0 + half * HALF, HALF), HALF)]

    @pl.when(diag)
    def _():
        for h in range(2):
            pltpu.make_async_copy(
                x_hbm.at[pl.ds(h * HALF, HALF)], block(0, h), x0_sem.at[h]
            ).start()
        pltpu.make_async_copy(wq_hbm_low, wq_low, w_sem.at[0]).start()
        pltpu.make_async_copy(wq_hbm_high, wq_high, w_sem.at[1]).start()
        pltpu.make_async_copy(wkv_hbm, wkv, w_sem.at[2]).start()

    barrier = pltpu.get_barrier_semaphore()

    def greet(n, carry):
        c2 = n // 16
        g2 = (n // 2) % 8
        y2 = n % 2
        mine = (c2 == core) & (g2 == rep) & (y2 == y)

        @pl.when(jnp.logical_not(mine))
        def _():
            pl.semaphore_signal(
                barrier, inc=1, device_id=dev(c2, g2, z, y2), device_id_type=pl.DeviceIdType.MESH
            )

        return carry

    lax.fori_loop(0, 32, greet, 0)
    for device in (up_dev, down_dev):
        pl.semaphore_signal(
            barrier, inc=1, device_id=device, device_id_type=pl.DeviceIdType.MESH
        )
    pl.semaphore_wait(barrier, 33)

    @pl.when(off)
    def _():
        for h in range(2):
            remote(
                x_hbm.at[pl.ds(h * HALF, HALF)],
                sibling_block(0, h),
                xs_send.at[h],
                x0_sem.at[h],
                swap_low,
            )
        remote(wq_hbm_high, wq_high, w_send.at[1], w_sem.at[1], swap_high)
        remote(wq_hbm_low, wq_low, w_send.at[0], w_sem.at[0], swap_low)
        remote(wkv_hbm, wkv, w_send.at[2], w_sem.at[2], swap_low)

    def send_up(src, dst, h, k):
        remote(block(src, h), block(dst, h), up_send.at[k], up_recv.at[k], up_dev)

    def send_down(src, dst, h, k):
        remote(block(src, h), block(dst, h), down_send.at[k], down_recv.at[k], down_dev)

    def share(slot, h):
        k = slot * 2 + h
        remote(block(slot, h), block(slot, h), sib_send.at[k], sib_recv.at[k], sibling)

    for h in range(2):
        landed(block(0, h), x0_sem.at[h])
        send_up(0, 1, h, h)
        send_down(0, 2, h, h)
        share(0, h)

    new_cols = pl.ds(CACHE, NEW)
    remote(new_ref, dec.at[y, new_cols], new_send.at[0], new_recv.at[0], across)
    dec[y, new_cols] = new_ref[...]

    def starts_of(rows, lens):
        end = jnp.int32(0)
        total = jnp.zeros_like(rows)
        for length in lens:
            end = end + length
            total = total + jnp.where(rows >= end, length, 0)
        return total

    work_lens = [lengths_ref[y, rep, j] for j in range(4)]
    home_lens = [lengths_ref[core, rep, j] for j in range(4)]
    paired = pairing_ref[core, rep]
    pair_lens = [lengths_ref[other, paired, j] for j in range(4)]

    def tables(plane, carry):
        rows = plane * PLANE_ROWS + lax.broadcasted_iota(jnp.int32, (PLANE_ROWS, HD), 0)
        lanes = lax.broadcasted_iota(jnp.int32, (PLANE_ROWS, HD), 1)
        offset = (rows - starts_of(rows, work_lens)).astype(jnp.float32)
        angle = offset * freq_ref[...]
        cos_t[plane] = jnp.cos(angle)
        sine = jnp.sin(angle)
        sin_t[plane] = jnp.where(lanes < HD // 2, -sine, sine)
        return carry

    lax.fori_loop(0, PLANES, tables, 0)

    def column(ref):
        spread = jnp.broadcast_to(ref[...], (ROWS, ROWS))
        here = lax.broadcasted_iota(jnp.int32, (ROWS, ROWS), 0) == lax.broadcasted_iota(
            jnp.int32, (ROWS, ROWS), 1
        )
        picked = jnp.where(here, spread.astype(jnp.float32), 0.0)
        return jnp.sum(picked, axis=1, keepdims=True).astype(jnp.int32)

    member = column(assign_ref)
    limit = column(cache_len_ref)
    lower = jnp.zeros_like(member)
    extent = jnp.zeros_like(member)
    begin = jnp.int32(0)
    for j in range(4):
        lower = jnp.where(member == j, begin, lower)
        extent = jnp.where(member == j, pair_lens[j], extent)
        begin = begin + pair_lens[j]
    upper = lower + jnp.minimum(extent, limit)
    spots = lax.broadcasted_iota(jnp.int32, (ROWS, CACHE), 1)
    visible = jnp.where((spots >= lower) & (spots < upper), 0.0, neg_large)
    new_spot = lax.broadcasted_iota(jnp.int32, (ROWS, NEW), 1)
    row = lax.broadcasted_iota(jnp.int32, (ROWS, NEW), 0)
    for s in range(STEPS):
        rows_here = pl.ds(s * ROWS, ROWS)
        bias[rows_here, pl.ds(0, CACHE)] = visible
        own = (new_spot % ROWS == row) & (new_spot // ROWS <= s)
        bias[rows_here, new_cols] = jnp.where(own, 0.0, neg_large)

    def relay(d, h):
        k = 2 * (d - 1) + h
        low, high = 2 * d - 1, 2 * d
        landed(block(low, h), up_recv.at[k])
        if d < 3:
            send_up(low, low + 2, h, k + 2)
        elif h == 0:
            send_up(low, low + 2, h, 6)
        share(low, h)
        landed(block(high, h), down_recv.at[k])
        if d < 3:
            send_down(high, high + 2, h, k + 2)
        elif h == 1:
            send_down(high, 7, h, 6)
        share(high, h)

    for d in (1, 2):
        for h in range(2):
            relay(d, h)
    relay(3, 0)
    landed(wq_low, w_sem.at[0])
    landed(wq_high, w_sem.at[1])
    landed(wkv, w_sem.at[2])

    def finish_plane(slot, plane, rows):
        cosine = cos_t[plane]
        sine = sin_t[plane]

        def turned(part):
            return part * cosine + pltpu.roll(part, HD // 2, 1) * sine

        heads = [turned(rows[:, h * HD : (h + 1) * HD]).astype(jnp.bfloat16) for h in range(HEADS)]
        raw = rows[:, HEADS * HD :]
        own = jnp.where(core == 0, turned(raw), raw).astype(jnp.bfloat16)
        kvstage[plane] = own

        @pl.when(diag)
        def _():
            for h in range(HEADS):
                qhome[plane, h] = heads[h]
            kvhome[core, plane] = own
            remote(
                kvstage.at[plane],
                kvhome.at[core, plane],
                kv_send.at[slot],
                kv_recv.at[core * PLANES + plane],
                across,
            )

        @pl.when(off)
        def _():
            for h in range(HEADS):
                qstage[slot, h] = heads[h]
            remote(
                kvstage.at[plane],
                kvhome.at[core, plane],
                kv_send.at[slot],
                kv_recv.at[core * PLANES + plane],
                swap_low,
            )
            remote(
                kvstage.at[plane],
                kvhome.at[core, plane],
                kv_send2.at[slot],
                kv_recv.at[core * PLANES + plane],
                sibling,
            )
            remote(qstage.at[slot], qhome.at[plane], q_send.at[slot], q_recv.at[plane], swap_low)

        @pl.when(plane == rep)
        def _():
            p1[rep] = own

        @pl.when(plane != rep)
        def _():
            remote(
                kvstage.at[plane],
                p1.at[rep],
                p1_send.at[slot],
                p1_recv.at[rep],
                dev(core, plane, z, y),
            )

    def project(b, carry):
        @pl.when(b == 2)
        def _():
            relay(3, 1)

        @pl.when(b == 3)
        def _():
            landed(block(7, 0), up_recv.at[6])
            share(7, 0)
            landed(block(7, 1), down_recv.at[6])
            share(7, 1)

        for j in range(2):
            for h in range(2):
                landed(sibling_block(2 * b + j, h), sib_recv.at[4 * b + 2 * j + h])

        acc[...] = jnp.zeros_like(acc)

        def step(k, inner):
            deep = pl.ds(pl.multiple_of(k * K_CHUNK, K_CHUNK), K_CHUNK)
            rows = xg[pl.ds(2 * b, 2), :, deep].reshape(2 * PLANE_ROWS, K_CHUNK)
            acc[:, : HEADS * HD] += jnp.dot(
                rows, wq[deep, :], preferred_element_type=jnp.float32
            )
            acc[:, HEADS * HD :] += jnp.dot(
                rows, wkv[deep, :], preferred_element_type=jnp.float32
            )
            return inner

        lax.fori_loop(0, wq.shape[0] // K_CHUNK, step, 0)
        finish_plane(2 * b, (z + b) % PLANES, acc[pl.ds(0, PLANE_ROWS), :])
        finish_plane(
            2 * b + 1, (z + 2 * PLANES - 1 - b) % PLANES, acc[pl.ds(PLANE_ROWS, PLANE_ROWS), :]
        )
        return carry

    lax.fori_loop(0, PLANES // 2, project, 0)

    for g2 in range(REPS):

        @pl.when(rep != g2)
        def _():
            landed(p1.at[g2], p1_recv.at[g2])

    cache_rows = pl.ds(pl.multiple_of(rep * PLANE_ROWS, PLANE_ROWS), PLANE_ROWS)

    def hand_over(d, carry):
        p2[d] = p1[pairing_ref[1 - y, d]]
        for y2 in range(2):
            mine = (1 - y == core) & (d == rep) & (y == y2)

            @pl.when(mine)
            def _():
                dec[core, cache_rows] = p2[d]

            @pl.when(jnp.logical_not(mine))
            def _():
                remote(
                    p2.at[d],
                    dec.at[core, cache_rows],
                    p2_send.at[2 * d + y2],
                    p2_recv.at[core * PLANES + rep],
                    dev(1 - y, d, z, y2),
                )

        return carry

    lax.fori_loop(0, REPS, hand_over, 0)

    for plane in range(PLANES):

        @pl.when(off)
        def _():
            landed(qhome.at[plane], q_recv.at[plane])
            landed(kvhome.at[0, plane], kv_recv.at[plane])
            landed(kvhome.at[1, plane], kv_recv.at[PLANES + plane])

        @pl.when(diag)
        def _():
            landed(kvhome.at[other, plane], kv_recv.at[other * PLANES + plane])

    def prefill(i, carry):
        first = jnp.maximum(i - (WINDOW - 1), 0)
        width = WINDOW * PLANE_ROWS
        keys = kvhome[0, pl.ds(first, WINDOW)].reshape(width, HD)
        values = kvhome[1, pl.ds(first, WINDOW)].reshape(width, HD)
        row_of = i * PLANE_ROWS + lax.broadcasted_iota(jnp.int32, (PLANE_ROWS, width), 0)
        spot = first * PLANE_ROWS + lax.broadcasted_iota(jnp.int32, (PLANE_ROWS, width), 1)
        begin_of = starts_of(row_of, home_lens)
        mask = jnp.where((spot >= begin_of) & (spot <= row_of), 0.0, neg_large)
        query = qhome[i].reshape(HEADS * PLANE_ROWS, HD)
        scores = scores_of(query, keys).reshape(HEADS, PLANE_ROWS, width) + mask[None]
        out = softmax_mix(scores.reshape(HEADS * PLANE_ROWS, width), values)
        rows_here = pl.ds(pl.multiple_of(i * PLANE_ROWS, PLANE_ROWS), PLANE_ROWS)
        for h in range(HEADS):
            prefill_ref[rows_here, h * HD : (h + 1) * HD] = out[
                h * PLANE_ROWS : (h + 1) * PLANE_ROWS
            ].astype(jnp.bfloat16)
        return carry

    lax.fori_loop(0, PLANES, prefill, 0)

    landed(dec.at[1 - y, new_cols], new_recv.at[0])
    for kind in range(2):
        for i in range(REPS):
            mine = (kind == core) & (i == rep) & (off)

            @pl.when(jnp.logical_not(mine))
            def _():
                landed(
                    dec.at[kind, pl.ds(i * PLANE_ROWS, PLANE_ROWS)], p2_recv.at[kind * PLANES + i]
                )

    for h in range(HEADS):
        scores = scores_of(queries_ref[:, h * HD : (h + 1) * HD], dec[0]) + bias[...]
        decode_ref[:, h * HD : (h + 1) * HD] = softmax_mix(scores, dec[1]).astype(jnp.bfloat16)

    landed(new_ref, new_send.at[0])
    for k in range(7):
        landed(block(0, 0), up_send.at[k])
        landed(block(0, 0), down_send.at[k])
    for k in range(16):
        landed(block(0, 0), sib_send.at[k])
    for slot in range(PLANES):
        landed(kvstage.at[0], kv_send.at[slot])

    @pl.when(off)
    def _():
        for h in range(2):
            landed(block(0, h), xs_send.at[h])
        landed(wq_low, w_send.at[0])
        landed(wq_high, w_send.at[1])
        landed(wkv, w_send.at[2])
        for slot in range(PLANES):
            landed(kvstage.at[0], kv_send2.at[slot])
            landed(qstage.at[0], q_send.at[slot])

    def drain(slot, carry):
        high = (z + slot // 2) % PLANES
        low = (z + 2 * PLANES - 1 - slot // 2) % PLANES
        plane = jnp.where(slot % 2 == 0, high, low)

        @pl.when(plane != rep)
        def _():
            landed(kvstage.at[0], p1_send.at[slot])

        for y2 in range(2):
            mine = (1 - y == core) & (slot == rep) & (y == y2)

            @pl.when(jnp.logical_not(mine))
            def _():
                landed(p2.at[0], p2_send.at[2 * slot + y2])

        return carry

    lax.fori_loop(0, PLANES, drain, 0)


def per_device(prompt_states, w_query, w_kv, queries, new_kv, lengths, pairing, assign, cache_len):
    depth = prompt_states.shape[-1]
    q_cols = w_query.shape[1]
    half = np.arange(HD // 2, dtype=np.float32) / np.float32(HD // 2)
    inverse = np.power(np.float32(theta_base), -half).astype(np.float32)
    freq = jnp.asarray(np.concatenate([inverse, inverse])[None, :])
    vmem = pl.BlockSpec(memory_space=pltpu.VMEM)
    smem = pl.BlockSpec(memory_space=pltpu.SMEM)
    anywhere = pl.BlockSpec(memory_space=pl.ANY)
    dma = pltpu.SemaphoreType.DMA
    bf16 = jnp.bfloat16
    prefill_out, decode_out = pl.pallas_call(
        kernel,
        out_shape=(
            jax.ShapeDtypeStruct((CACHE, q_cols), bf16),
            jax.ShapeDtypeStruct((NEW, q_cols), bf16),
        ),
        in_specs=[anywhere, anywhere, anywhere, vmem, vmem, smem, smem, vmem, vmem, vmem],
        out_specs=(vmem, vmem),
        scratch_shapes=[
            pltpu.VMEM((PLANES, PLANE_ROWS, depth), bf16),
            pltpu.VMEM((depth, q_cols), bf16),
            pltpu.VMEM((depth, HD), bf16),
            pltpu.VMEM((2 * PLANE_ROWS, q_cols + HD), jnp.float32),
            pltpu.VMEM((PLANES, PLANE_ROWS, HD), jnp.float32),
            pltpu.VMEM((PLANES, PLANE_ROWS, HD), jnp.float32),
            pltpu.VMEM((NEW, CACHE + NEW), jnp.float32),
            pltpu.VMEM((PLANES, HEADS, PLANE_ROWS, HD), bf16),
            pltpu.VMEM((PLANES, HEADS, PLANE_ROWS, HD), bf16),
            pltpu.VMEM((2, PLANES, PLANE_ROWS, HD), bf16),
            pltpu.VMEM((PLANES, PLANE_ROWS, HD), bf16),
            pltpu.VMEM((REPS, PLANE_ROWS, HD), bf16),
            pltpu.VMEM((REPS, PLANE_ROWS, HD), bf16),
            pltpu.VMEM((2, CACHE + NEW, HD), bf16),
            dma((2,)),
            dma((2,)),
            dma((3,)),
            dma((3,)),
            dma((7,)),
            dma((7,)),
            dma((7,)),
            dma((7,)),
            dma((16,)),
            dma((16,)),
            dma((1,)),
            dma((1,)),
            dma((PLANES,)),
            dma((PLANES,)),
            dma((PLANES,)),
            dma((PLANES,)),
            dma((2 * PLANES,)),
            dma((PLANES,)),
            dma((REPS,)),
            dma((2 * REPS,)),
            dma((2 * REPS,)),
        ],
        compiler_params=pltpu.CompilerParams(
            collective_id=0, has_side_effects=True, vmem_limit_bytes=56 * 1024 * 1024
        ),
        cost_estimate=pl.CostEstimate(
            flops=2 * CACHE * depth * (q_cols + HD) + 8 * CACHE * CACHE * q_cols,
            bytes_accessed=2 * depth * (q_cols + HD + TOK),
            transcendentals=2 * HEADS * CACHE * CACHE,
        ),
    )(
        prompt_states.reshape(TOK, depth),
        w_query,
        w_kv,
        queries.reshape(NEW, q_cols),
        new_kv.reshape(NEW, HD),
        lengths,
        pairing,
        assign.reshape(1, ROWS),
        cache_len.reshape(1, ROWS),
        freq,
    )
    return (
        prefill_out.reshape(1, 1, CACHE, q_cols),
        decode_out.reshape(1, 1, STEPS, ROWS, q_cols),
    )


def solution(mesh):
    placed = (
        P("pool", "rep", "tp", None),
        P(None, "tp"),
        P(None, "tp"),
        P("pool", "rep", None, None, "tp"),
        P("pool", "rep", None, None, "tp"),
        P(),
        P(),
        P("pool", "rep", None),
        P("pool", "rep", None),
    )
    return jax.shard_map(
        per_device,
        mesh=mesh,
        in_specs=placed,
        out_specs=(P("pool", "rep", None, "tp"), P("pool", "rep", None, None, "tp")),
        check_vma=False,
    )
```

time: 515 us -> 132 us (0.26); the launches traced: 510 us -> 132 us
  waiting for transfers between devices: 394 us -> 0 us
  Pallas kernels: 0 us -> 126 us
  matrix products: 46.2 us -> 0 us
  other arithmetic: 25.4 us -> 0 us
  local copies, waits for them, and re-layouts: 27.4 us -> 5.3 us
  between operations: 15.4 us -> 0.64 us
    all_gather x2 -> x0, waiting for transfers between devices: 387 us -> none  [the longest x1 353 us: per_device(): shard_rows = lax.all_gather(local_rows, 'tp', axis=0, tiled=True)]
    pallas_call x0 -> x1, Pallas kernels: none -> 126 us  [per_device(): pl.pallas_call(kernel, out_shape=(jax.ShapeDtypeStruct((CACHE, q_cols), b...]
    dot_general x8 -> x0, matrix products: 46.2 us -> none  [the longest x1 17.3 us: per_device(): jnp.dot(shard_rows, w_query, preferred_element_type=jnp.float32)]
    unnamed x30 -> x3, local copies, waits for them, and re-layouts: 22.5 us -> 5.3 us
    reduce_sum x9 -> x0, other arithmetic: 14.6 us -> none  [the longest x1 6.08 us: hand_over(): jnp.sum(jnp.where(member, shard_rows, jnp.zeros_like(shard_rows)), axis=0)]
    ppermute x2 -> x0, waiting for transfers between devices: 7.16 us -> none  [from_partner(): return lax.ppermute(block, axis, route)]
  transfers between devices with their start and end apart: 4 -> 0, of which waited for: 3 -> 0; matrix products, arithmetic and copies ran while one was open for 10% -> 0% of each run, Pallas kernels for 0% -> 0%
where the time goes in v1:
time: 132 us
  Pallas kernels  126 us (95%)
  local copies, waits for them, and re-layouts  5.3 us (4%)
    pallas_call x1, Pallas kernels, per_device(): pl.pallas_call(kernel, out_shape=(jax.ShapeDtypeStruct((CACHE, q_cols), b...  126 us
    unnamed x3, local copies, waits for them, and re-layouts  5.3 us

profile of v1, /device:TPU:1, one launch (start us, length us, event | category | flops | bytes accessed | tf_op | source)
XLA Modules:
  0.0 132.1 jit_solution(12587258100299386942)
XLA Ops:
  0.6 1.4 %copy.12.lengths_ref = s32[2,8,4]{2,1,0:T(8,128)} copy(s32[2,8,4]{1,2,0:T(4,128)} %param.15) | data formatting | bytes 512 | tf_op args[5]
  2.0 126.1 %shard_map.113 = (bf16[1024,512]{1,0:T(8,128)(2,1)}, bf16[256,512]{1,0:T(8,128)(2,1)}) custom-call(bf16[64,8192]{1,0:T(8,128)(2,1)} %bitcast.9, bf16[8192,512]{1,0:T(8,128)(2,1)} %wq_hbm.1, bf16[8192,128]{1,0:T(8,128)(2,1)} %wkv_hbm.1, bf16[256,512]{1,0:T(8,128)(2,1)} %bitcast.10, bf16[256,128]{1,0:T(8,128)(2,1)} %bitcast.11, s32[2,8,4]{2,1,0:T(8,128)} %copy.12.lengths_ref, ...), custom_call_target="tpu_custom_call" | custom-call | flops 15032385536 | bytes 11534336 | tf_op jit(solution)/shard_map/pallas_call | solution.py:514
  128.1 2.3 %copy.15 = bf16[1,1,1024,512]{3,2,1,0:T(8,128)(2,1)} copy(bf16[1,1,1024,512]{3,2,1,0:T(8,128)(2,1)} %bitcast.7) | data formatting | bytes 2097152
  130.4 1.7 %copy.16 = bf16[1,1,4,64,512]{4,3,2,1,0:T(8,128)(2,1)} copy(bf16[1,1,4,64,512]{4,3,2,1,0:T(8,128)(2,1)} %bitcast.8) | data formatting | bytes 524288

commit v2 on v1

--- a/solution.py
+++ b/solution.py
@@ -14,15 +14,17 @@
 REPS = 8
 HEADS = 4
 TOK = 64
-HALF = 32
 PLANE_ROWS = 2 * TOK
 WINDOW = 5
 STEPS = 4
 ROWS = 64
 NEW = STEPS * ROWS
 CACHE = PLANES * PLANE_ROWS
-W_LOW = 2560
-K_CHUNK = 2048
+W_PIECE = 256
+W_LOW_PIECES = 3
+W_PIECES = 8
+N_TILE = 256
+WORK = HEADS * PLANE_ROWS
 
 theta_base = 500000.0
 neg_large = -1e30
@@ -42,14 +44,6 @@
 
 def landed(ref, sem):
     pltpu.make_async_copy(ref, ref, sem).wait()
-
-
-def softmax_mix(scores, values):
-    peak = jnp.max(scores, axis=-1, keepdims=True)
-    weights = jnp.exp2((scores - peak) * exp_scale)
-    total = jnp.sum(weights, axis=-1, keepdims=True)
-    mixed = jnp.dot(weights.astype(jnp.bfloat16), values, preferred_element_type=jnp.float32)
-    return mixed / total
 
 
 def scores_of(query, keys):
@@ -72,9 +66,9 @@
     prefill_ref,
     decode_ref,
     xg,
-    wq,
-    wkv,
-    acc,
+    wall,
+    accs,
+    partial,
     cos_t,
     sin_t,
     bias,
@@ -85,16 +79,27 @@
     p1,
     p2,
     dec,
+    top,
+    total,
+    mix,
+    dec_top,
+    dec_total,
+    dec_mix,
     x0_sem,
     xs_send,
-    w_sem,
-    w_send,
+    wl_sem,
+    wq_send,
+    wq_recv,
+    wkv_send,
+    wkv_recv,
+    wx_send,
+    wx_recv,
     up_send,
     up_recv,
     down_send,
     down_recv,
-    sib_send,
-    sib_recv,
+    part_send,
+    part_recv,
     new_send,
     new_recv,
     q_send,
@@ -123,31 +128,57 @@
     down_dev = dev(core, rep, (z + PLANES - 1) % PLANES, y)
     sibling = dev(other, rep, z, y)
     swap_low = dev(other, rep, z, 1 - y)
-    swap_high = dev(other, (rep + REPS // 2) % REPS, z, 1 - y)
     across = dev(core, rep, z, 1 - y)
-    row0 = pl.multiple_of(core * TOK, TOK)
-    other_row0 = pl.multiple_of(other * TOK, TOK)
-
-    wq_low = wq.at[pl.ds(0, W_LOW)]
-    wq_high = wq.at[pl.ds(W_LOW, wq.shape[0] - W_LOW)]
-    wq_hbm_low = wq_hbm.at[pl.ds(0, W_LOW)]
-    wq_hbm_high = wq_hbm.at[pl.ds(W_LOW, wq.shape[0] - W_LOW)]
-
-    def block(slot, half):
-        return xg.at[slot, pl.ds(pl.multiple_of(row0 + half * HALF, HALF), HALF)]
-
-    def sibling_block(slot, half):
-        return xg.at[slot, pl.ds(pl.multiple_of(other_row0 + half * HALF, HALF), HALF)]
+    across_high = dev(core, (rep + REPS // 2) % REPS, z, 1 - y)
+    q_cols = wq_hbm.shape[1]
+    parity = rep % 2
+    row_of_x = rep // 4 * 4
+    right = dev(core, row_of_x + (rep + 1) % 4, z, y)
+    left = dev(core, row_of_x + (rep + 3) % 4, z, y)
+    half_depth = W_PIECES * W_PIECE
+
+    depth = wall.shape[0]
+    cols = q_cols + HD
+    own_depth = pl.multiple_of(core * depth, depth)
+    other_depth = pl.multiple_of(other * depth, depth)
+    mine_cols = pl.ds(pl.multiple_of(core * cols, HD), cols)
+    sibling_cols = pl.ds(pl.multiple_of(other * cols, HD), cols)
+    far_cols = pl.ds(pl.multiple_of((1 - y) * cols, HD), cols)
+    far_q_cols = pl.ds(pl.multiple_of((1 - y) * cols, HD), q_cols)
+    far_kv_cols = pl.ds(pl.multiple_of((1 - y) * cols + q_cols, HD), HD)
+    near_q_cols = pl.ds(pl.multiple_of(y * cols, HD), q_cols)
+    near_kv_cols = pl.ds(pl.multiple_of(y * cols + q_cols, HD), HD)
+    half_depth = W_PIECES * W_PIECE
+
+    def depth_rows(half, n):
+        return pl.ds(pl.multiple_of(half * half_depth + n * W_PIECE, W_PIECE), W_PIECE)
+
+    def source_rows(half, n):
+        start = core * depth + half * half_depth + n * W_PIECE
+        return pl.ds(pl.multiple_of(start, W_PIECE), W_PIECE)
+
+    def distance(plane):
+        away = (plane + PLANES - z) % PLANES
+        return jnp.minimum(away, PLANES - away)
+
+    y_rows = pl.ds(pl.multiple_of(y * TOK, TOK), TOK)
+    far_rows = pl.ds(pl.multiple_of((1 - y) * TOK, TOK), TOK)
+
+    def block(slot, h):
+        return xg.at[slot, y_rows if h == 0 else far_rows]
 
     @pl.when(diag)
     def _():
-        for h in range(2):
-            pltpu.make_async_copy(
-                x_hbm.at[pl.ds(h * HALF, HALF)], block(0, h), x0_sem.at[h]
-            ).start()
-        pltpu.make_async_copy(wq_hbm_low, wq_low, w_sem.at[0]).start()
-        pltpu.make_async_copy(wq_hbm_high, wq_high, w_sem.at[1]).start()
-        pltpu.make_async_copy(wkv_hbm, wkv, w_sem.at[2]).start()
+        pltpu.make_async_copy(
+            x_hbm.at[:, pl.ds(own_depth, depth)], xg.at[0, y_rows], x0_sem.at[0]
+        ).start()
+
+    pltpu.make_async_copy(
+        wq_hbm.at[pl.ds(own_depth, depth)], wall.at[:, near_q_cols], wl_sem.at[0]
+    ).start()
+    pltpu.make_async_copy(
+        wkv_hbm.at[pl.ds(own_depth, depth)], wall.at[:, near_kv_cols], wl_sem.at[1]
+    ).start()
 
     barrier = pltpu.get_barrier_semaphore()
 
@@ -172,35 +203,69 @@
         )
     pl.semaphore_wait(barrier, 33)
 
+    @pl.when(diag)
+    def _():
+        remote(
+            x_hbm.at[:, pl.ds(other_depth, depth)],
+            xg.at[0, y_rows],
+            xs_send.at[0],
+            x0_sem.at[0],
+            sibling,
+        )
+
     @pl.when(off)
     def _():
-        for h in range(2):
-            remote(
-                x_hbm.at[pl.ds(h * HALF, HALF)],
-                sibling_block(0, h),
-                xs_send.at[h],
-                x0_sem.at[h],
-                swap_low,
-            )
-        remote(wq_hbm_high, wq_high, w_send.at[1], w_sem.at[1], swap_high)
-        remote(wq_hbm_low, wq_low, w_send.at[0], w_sem.at[0], swap_low)
-        remote(wkv_hbm, wkv, w_send.at[2], w_sem.at[2], swap_low)
+        remote(
+            x_hbm.at[:, pl.ds(own_depth, depth)],
+            xg.at[0, y_rows],
+            xs_send.at[0],
+            x0_sem.at[1],
+            across,
+        )
+        remote(
+            x_hbm.at[:, pl.ds(other_depth, depth)],
+            xg.at[0, y_rows],
+            xs_send.at[1],
+            x0_sem.at[1],
+            swap_low,
+        )
+
+    for n in range(W_PIECES):
+        target = across if n < W_LOW_PIECES else across_high
+        remote(
+            wq_hbm.at[source_rows(parity, n)],
+            wall.at[depth_rows(parity, n), near_q_cols],
+            wq_send.at[n],
+            wq_recv.at[n],
+            target,
+        )
+        remote(
+            wkv_hbm.at[source_rows(parity, n)],
+            wall.at[depth_rows(parity, n), near_kv_cols],
+            wkv_send.at[n],
+            wkv_recv.at[n],
+            target,
+        )
+
+    def pass_on(pieces):
+        for n in pieces:
+            rows = depth_rows(parity, n)
+            landed(wall.at[rows, far_q_cols], wq_recv.at[n])
+            landed(wall.at[rows, far_kv_cols], wkv_recv.at[n])
+            target = right if n < W_LOW_PIECES else left
+            piece = wall.at[rows, far_cols]
+            remote(piece, piece, wx_send.at[n], wx_recv.at[n], target)
 
     def send_up(src, dst, h, k):
         remote(block(src, h), block(dst, h), up_send.at[k], up_recv.at[k], up_dev)
 
     def send_down(src, dst, h, k):
         remote(block(src, h), block(dst, h), down_send.at[k], down_recv.at[k], down_dev)
-
-    def share(slot, h):
-        k = slot * 2 + h
-        remote(block(slot, h), block(slot, h), sib_send.at[k], sib_recv.at[k], sibling)
 
     for h in range(2):
         landed(block(0, h), x0_sem.at[h])
         send_up(0, 1, h, h)
         send_down(0, 2, h, h)
-        share(0, h)
 
     new_cols = pl.ds(CACHE, NEW)
     remote(new_ref, dec.at[y, new_cols], new_send.at[0], new_recv.at[0], across)
@@ -214,10 +279,10 @@
             total = total + jnp.where(rows >= end, length, 0)
         return total
 
-    work_lens = [lengths_ref[y, rep, j] for j in range(4)]
-    home_lens = [lengths_ref[core, rep, j] for j in range(4)]
+    work_lens = [lengths_ref[y, j, rep] for j in range(4)]
+    home_lens = [lengths_ref[core, j, rep] for j in range(4)]
     paired = pairing_ref[core, rep]
-    pair_lens = [lengths_ref[other, paired, j] for j in range(4)]
+    pair_lens = [lengths_ref[other, j, paired] for j in range(4)]
 
     def tables(plane, carry):
         rows = plane * PLANE_ROWS + lax.broadcasted_iota(jnp.int32, (PLANE_ROWS, HD), 0)
@@ -267,21 +332,11 @@
             send_up(low, low + 2, h, k + 2)
         elif h == 0:
             send_up(low, low + 2, h, 6)
-        share(low, h)
         landed(block(high, h), down_recv.at[k])
         if d < 3:
             send_down(high, high + 2, h, k + 2)
         elif h == 1:
             send_down(high, 7, h, 6)
-        share(high, h)
-
-    for d in (1, 2):
-        for h in range(2):
-            relay(d, h)
-    relay(3, 0)
-    landed(wq_low, w_sem.at[0])
-    landed(wq_high, w_sem.at[1])
-    landed(wkv, w_sem.at[2])
 
     def finish_plane(slot, plane, rows):
         cosine = cos_t[plane]
@@ -342,76 +397,70 @@
                 dev(core, plane, z, y),
             )
 
-    def project(b, carry):
-        @pl.when(b == 2)
+    def project(first, count):
+        rows_here = count * PLANE_ROWS
+
+        def tile(n, carry):
+            wide = pl.ds(pl.multiple_of(n * N_TILE, N_TILE), N_TILE)
+            rows = xg[pl.ds(first, count)].reshape(rows_here, depth)
+            out = jnp.dot(rows, wall[:, wide], preferred_element_type=jnp.float32)
+            accs[pl.ds(first, count), :, wide] = out.reshape(count, PLANE_ROWS, N_TILE)
+            return carry
+
+        lax.fori_loop(0, wall.shape[1] // N_TILE, tile, 0)
+        for slot in range(first, first + count):
+            remote(
+                accs.at[slot, :, sibling_cols],
+                partial.at[slot],
+                part_send.at[slot],
+                part_recv.at[slot],
+                sibling,
+            )
+
+    def finish(slots):
+        for slot, away in slots:
+            landed(partial.at[slot], part_recv.at[slot])
+            rows = accs[slot, :, mine_cols] + partial[slot]
+            finish_plane(slot, (z + PLANES + away) % PLANES, rows)
+
+    cache_rows = pl.ds(pl.multiple_of(rep * PLANE_ROWS, PLANE_ROWS), PLANE_ROWS)
+
+    def hand_over(nearest, farthest):
+        here = distance(rep)
+
+        @pl.when((here >= nearest) & (here <= farthest))
         def _():
-            relay(3, 1)
-
-        @pl.when(b == 3)
-        def _():
-            landed(block(7, 0), up_recv.at[6])
-            share(7, 0)
-            landed(block(7, 1), down_recv.at[6])
-            share(7, 1)
-
-        for j in range(2):
-            for h in range(2):
-                landed(sibling_block(2 * b + j, h), sib_recv.at[4 * b + 2 * j + h])
-
-        acc[...] = jnp.zeros_like(acc)
-
-        def step(k, inner):
-            deep = pl.ds(pl.multiple_of(k * K_CHUNK, K_CHUNK), K_CHUNK)
-            rows = xg[pl.ds(2 * b, 2), :, deep].reshape(2 * PLANE_ROWS, K_CHUNK)
-            acc[:, : HEADS * HD] += jnp.dot(
-                rows, wq[deep, :], preferred_element_type=jnp.float32
-            )
-            acc[:, HEADS * HD :] += jnp.dot(
-                rows, wkv[deep, :], preferred_element_type=jnp.float32
-            )
-            return inner
-
-        lax.fori_loop(0, wq.shape[0] // K_CHUNK, step, 0)
-        finish_plane(2 * b, (z + b) % PLANES, acc[pl.ds(0, PLANE_ROWS), :])
-        finish_plane(
-            2 * b + 1, (z + 2 * PLANES - 1 - b) % PLANES, acc[pl.ds(PLANE_ROWS, PLANE_ROWS), :]
-        )
-        return carry
-
-    lax.fori_loop(0, PLANES // 2, project, 0)
-
-    for g2 in range(REPS):
-
-        @pl.when(rep != g2)
-        def _():
-            landed(p1.at[g2], p1_recv.at[g2])
-
-    cache_rows = pl.ds(pl.multiple_of(rep * PLANE_ROWS, PLANE_ROWS), PLANE_ROWS)
-
-    def hand_over(d, carry):
-        p2[d] = p1[pairing_ref[1 - y, d]]
-        for y2 in range(2):
-            mine = (1 - y == core) & (d == rep) & (y == y2)
-
-            @pl.when(mine)
-            def _():
-                dec[core, cache_rows] = p2[d]
-
-            @pl.when(jnp.logical_not(mine))
-            def _():
-                remote(
-                    p2.at[d],
-                    dec.at[core, cache_rows],
-                    p2_send.at[2 * d + y2],
-                    p2_recv.at[core * PLANES + rep],
-                    dev(1 - y, d, z, y2),
-                )
-
-        return carry
-
-    lax.fori_loop(0, REPS, hand_over, 0)
-
-    for plane in range(PLANES):
+            for g2 in range(REPS):
+
+                @pl.when(rep != g2)
+                def _():
+                    landed(p1.at[g2], p1_recv.at[g2])
+
+            def give(d, carry):
+                p2[d] = p1[pairing_ref[1 - y, d]]
+                for y2 in range(2):
+                    mine = (1 - y == core) & (d == rep) & (y == y2)
+
+                    @pl.when(mine)
+                    def _():
+                        dec[core, cache_rows] = p2[d]
+
+                    @pl.when(jnp.logical_not(mine))
+                    def _():
+                        remote(
+                            p2.at[d],
+                            dec.at[core, cache_rows],
+                            p2_send.at[2 * d + y2],
+                            p2_recv.at[core * PLANES + rep],
+                            dev(1 - y, d, z, y2),
+                        )
+
+                return carry
+
+            lax.fori_loop(0, REPS, give, 0)
+
+    def home_landed(away):
+        plane = (z + PLANES + away) % PLANES
 
         @pl.when(off)
         def _():
@@ -423,66 +472,215 @@
         def _():
             landed(kvhome.at[other, plane], kv_recv.at[other * PLANES + plane])
 
-    def prefill(i, carry):
-        first = jnp.maximum(i - (WINDOW - 1), 0)
-        width = WINDOW * PLANE_ROWS
-        keys = kvhome[0, pl.ds(first, WINDOW)].reshape(width, HD)
-        values = kvhome[1, pl.ds(first, WINDOW)].reshape(width, HD)
-        row_of = i * PLANE_ROWS + lax.broadcasted_iota(jnp.int32, (PLANE_ROWS, width), 0)
-        spot = first * PLANE_ROWS + lax.broadcasted_iota(jnp.int32, (PLANE_ROWS, width), 1)
+    def attend(i, planes, fresh):
+        width = len(planes) * PLANE_ROWS
+        row_of = i * PLANE_ROWS + lax.broadcasted_iota(jnp.int32, (PLANE_ROWS, 1), 0)
+        lanes = lax.broadcasted_iota(jnp.int32, (PLANE_ROWS, PLANE_ROWS), 1)
+        spot = jnp.concatenate([lanes + j * PLANE_ROWS for j in planes], axis=1)
+        keys = jnp.concatenate([kvhome[0, j] for j in planes], axis=0)
+        values = jnp.concatenate([kvhome[1, j] for j in planes], axis=0)
         begin_of = starts_of(row_of, home_lens)
         mask = jnp.where((spot >= begin_of) & (spot <= row_of), 0.0, neg_large)
-        query = qhome[i].reshape(HEADS * PLANE_ROWS, HD)
-        scores = scores_of(query, keys).reshape(HEADS, PLANE_ROWS, width) + mask[None]
-        out = softmax_mix(scores.reshape(HEADS * PLANE_ROWS, width), values)
-        rows_here = pl.ds(pl.multiple_of(i * PLANE_ROWS, PLANE_ROWS), PLANE_ROWS)
+        scores = scores_of(qhome[i].reshape(WORK, HD), keys)
+        scores = (scores.reshape(HEADS, PLANE_ROWS, width) + mask[None]).reshape(WORK, width)
+        peak = jnp.max(scores, axis=-1, keepdims=True)
+        if not fresh:
+            before = top[i]
+            peak = jnp.maximum(before[:, :1], peak)
+            fade = jnp.exp2((before - peak) * exp_scale)
+        weights = jnp.exp2((scores - peak) * exp_scale)
+        summed = jnp.sum(weights, axis=-1, keepdims=True)
+        mixed = jnp.dot(weights.astype(jnp.bfloat16), values, preferred_element_type=jnp.float32)
+        if fresh:
+            total[i] = jnp.broadcast_to(summed, (WORK, HD))
+            mix[i] = mixed
+        else:
+            total[i] = total[i] * fade + summed
+            mix[i] = mix[i] * fade + mixed
+        top[i] = jnp.broadcast_to(peak, (WORK, HD))
+
+    def plane_at(away):
+        return (z + PLANES + away) % PLANES
+
+    def attend_near():
+        planes = [plane_at(away) for away in near]
+
+        def one(n, carry):
+            attend((z + PLANES - 2 + n) % PLANES, planes, True)
+            return carry
+
+        lax.fori_loop(0, 5, one, 0)
+
+    def attend_third():
+        planes = [plane_at(-3), plane_at(3)]
+
+        def one(n, carry):
+            attend((z + PLANES - 2 + n) % PLANES, planes, False)
+            return carry
+
+        lax.fori_loop(0, 5, one, 0)
+
+        def two(n, carry):
+            attend((z + PLANES - 3 + 6 * n) % PLANES, planes + [plane_at(a) for a in near], True)
+            return carry
+
+        lax.fori_loop(0, 2, two, 0)
+
+    def attend_last():
+        last = plane_at(4)
+        first = jnp.maximum(last - (WINDOW - 1), 0)
+        attend(last, [first + n for n in range(WINDOW)], True)
+
+        def one(n, carry):
+            i = last + 1 + n
+
+            @pl.when(i < PLANES)
+            def _():
+                attend(i, [last], False)
+
+            return carry
+
+        lax.fori_loop(0, WINDOW - 1, one, 0)
+
+    def settle(late):
+        def one(i, carry):
+            after = i - (z + 4) % PLANES
+            needs_last = (after >= 0) & (after < WINDOW)
+
+            @pl.when(needs_last if late else jnp.logical_not(needs_last))
+            def _():
+                out = mix[i] / total[i]
+                rows_here = pl.ds(pl.multiple_of(i * PLANE_ROWS, PLANE_ROWS), PLANE_ROWS)
+                for h in range(HEADS):
+                    prefill_ref[rows_here, h * HD : (h + 1) * HD] = out[
+                        h * PLANE_ROWS : (h + 1) * PLANE_ROWS
+                    ].astype(jnp.bfloat16)
+
+            return carry
+
+        lax.fori_loop(0, PLANES, one, 0)
+
+    def caches_landed(aways):
+        for away in aways:
+            plane = (z + PLANES + away) % PLANES
+            rows_here = pl.ds(pl.multiple_of(plane * PLANE_ROWS, PLANE_ROWS), PLANE_ROWS)
+            for kind in range(2):
+                mine = (kind == core) & (plane == rep) & off
+
+                @pl.when(jnp.logical_not(mine))
+                def _():
+                    landed(dec.at[kind, rows_here], p2_recv.at[kind * PLANES + plane])
+
+    def cache_slices(aways):
+        slices = []
+        for away in aways:
+            plane = (z + PLANES + away) % PLANES
+            slices.append(pl.ds(pl.multiple_of(plane * PLANE_ROWS, PLANE_ROWS), PLANE_ROWS))
+        return slices
+
+    def decode_scores(h, slices):
+        query = queries_ref[:, h * HD : (h + 1) * HD]
+        keys = jnp.concatenate([dec[0, piece] for piece in slices], axis=0)
+        mask = jnp.concatenate([bias[:, piece] for piece in slices], axis=1)
+        values = jnp.concatenate([dec[1, piece] for piece in slices], axis=0)
+        return scores_of(query, keys) + mask, values
+
+    def decode_first(aways):
+        slices = cache_slices(aways) + [new_cols]
         for h in range(HEADS):
-            prefill_ref[rows_here, h * HD : (h + 1) * HD] = out[
-                h * PLANE_ROWS : (h + 1) * PLANE_ROWS
-            ].astype(jnp.bfloat16)
-        return carry
-
-    lax.fori_loop(0, PLANES, prefill, 0)
-
+            scores, values = decode_scores(h, slices)
+            peak = jnp.max(scores, axis=-1, keepdims=True)
+            weights = jnp.exp2((scores - peak) * exp_scale)
+            dec_top[h] = jnp.broadcast_to(peak, (NEW, HD))
+            dec_total[h] = jnp.broadcast_to(
+                jnp.sum(weights, axis=-1, keepdims=True), (NEW, HD)
+            )
+            dec_mix[h] = jnp.dot(
+                weights.astype(jnp.bfloat16), values, preferred_element_type=jnp.float32
+            )
+
+    def decode_last(aways):
+        slices = cache_slices(aways)
+        for h in range(HEADS):
+            scores, values = decode_scores(h, slices)
+            before = dec_top[h]
+            peak = jnp.maximum(before, jnp.max(scores, axis=-1, keepdims=True))
+            fade = jnp.exp2((before - peak) * exp_scale)
+            weights = jnp.exp2((scores - peak[:, :1]) * exp_scale)
+            whole = dec_total[h] * fade + jnp.sum(weights, axis=-1, keepdims=True)
+            mixed = dec_mix[h] * fade + jnp.dot(
+                weights.astype(jnp.bfloat16), values, preferred_element_type=jnp.float32
+            )
+            decode_ref[:, h * HD : (h + 1) * HD] = (mixed / whole).astype(jnp.bfloat16)
+
+    near = (0, -1, 1, -2, 2)
+    relay(1, 0)
+    pass_on((3, 4))
+    relay(1, 1)
+    pass_on((0, 5, 1, 6))
+    relay(2, 0)
+    pass_on((2, 7))
+    relay(2, 1)
+    landed(wall.at[:, near_q_cols], wl_sem.at[0])
+    landed(wall.at[:, near_kv_cols], wl_sem.at[1])
+    for n in range(W_PIECES):
+        landed(wall.at[depth_rows(1 - parity, n), far_cols], wx_recv.at[n])
+
+    project(0, 5)
+    relay(3, 0)
+    finish(((0, 0), (1, -1), (2, 1), (3, -2), (4, 2)))
+    hand_over(0, 2)
+    for away in near:
+        home_landed(away)
+    attend_near()
+    relay(3, 1)
+    project(5, 2)
     landed(dec.at[1 - y, new_cols], new_recv.at[0])
-    for kind in range(2):
-        for i in range(REPS):
-            mine = (kind == core) & (i == rep) & (off)
-
-            @pl.when(jnp.logical_not(mine))
-            def _():
-                landed(
-                    dec.at[kind, pl.ds(i * PLANE_ROWS, PLANE_ROWS)], p2_recv.at[kind * PLANES + i]
-                )
-
-    for h in range(HEADS):
-        scores = scores_of(queries_ref[:, h * HD : (h + 1) * HD], dec[0]) + bias[...]
-        decode_ref[:, h * HD : (h + 1) * HD] = softmax_mix(scores, dec[1]).astype(jnp.bfloat16)
+    caches_landed(near)
+    decode_first(near)
+    finish(((5, -3), (6, 3)))
+    hand_over(3, 3)
+    for away in (-3, 3):
+        home_landed(away)
+    attend_third()
+    settle(False)
+    landed(block(7, 0), up_recv.at[6])
+    landed(block(7, 1), down_recv.at[6])
+    project(7, 1)
+    finish(((7, 4),))
+    hand_over(4, 4)
+    home_landed(4)
+    attend_last()
+    settle(True)
+    far = (-3, 3, 4)
+    caches_landed(far)
+    decode_last(far)
 
     landed(new_ref, new_send.at[0])
     for k in range(7):
         landed(block(0, 0), up_send.at[k])
         landed(block(0, 0), down_send.at[k])
-    for k in range(16):
-        landed(block(0, 0), sib_send.at[k])
+    landed(block(0, 0), xs_send.at[0])
     for slot in range(PLANES):
         landed(kvstage.at[0], kv_send.at[slot])
+        landed(partial.at[0], part_send.at[slot])
+    for n in range(W_PIECES):
+        rows = depth_rows(0, n)
+        landed(wall.at[rows, near_q_cols], wq_send.at[n])
+        landed(wall.at[rows, near_kv_cols], wkv_send.at[n])
+        landed(wall.at[rows, far_cols], wx_send.at[n])
 
     @pl.when(off)
     def _():
-        for h in range(2):
-            landed(block(0, h), xs_send.at[h])
-        landed(wq_low, w_send.at[0])
-        landed(wq_high, w_send.at[1])
-        landed(wkv, w_send.at[2])
+        landed(block(0, 0), xs_send.at[1])
         for slot in range(PLANES):
             landed(kvstage.at[0], kv_send2.at[slot])
             landed(qstage.at[0], q_send.at[slot])
 
     def drain(slot, carry):
-        high = (z + slot // 2) % PLANES
-        low = (z + 2 * PLANES - 1 - slot // 2) % PLANES
-        plane = jnp.where(slot % 2 == 0, high, low)
+        odd = slot % 2
+        step = (slot + odd) // 2
+        plane = jnp.where(odd == 0, (z + step) % PLANES, (z + PLANES - step) % PLANES)
 
         @pl.when(plane != rep)
         def _():
@@ -520,10 +718,10 @@
         in_specs=[anywhere, anywhere, anywhere, vmem, vmem, smem, smem, vmem, vmem, vmem],
         out_specs=(vmem, vmem),
         scratch_shapes=[
-            pltpu.VMEM((PLANES, PLANE_ROWS, depth), bf16),
-            pltpu.VMEM((depth, q_cols), bf16),
-            pltpu.VMEM((depth, HD), bf16),
-            pltpu.VMEM((2 * PLANE_ROWS, q_cols + HD), jnp.float32),
+            pltpu.VMEM((PLANES, PLANE_ROWS, depth // 2), bf16),
+            pltpu.VMEM((depth // 2, 2 * (q_cols + HD)), bf16),
+            pltpu.VMEM((PLANES, PLANE_ROWS, 2 * (q_cols + HD)), jnp.float32),
+            pltpu.VMEM((PLANES, PLANE_ROWS, q_cols + HD), jnp.float32),
             pltpu.VMEM((PLANES, PLANE_ROWS, HD), jnp.float32),
             pltpu.VMEM((PLANES, PLANE_ROWS, HD), jnp.float32),
             pltpu.VMEM((NEW, CACHE + NEW), jnp.float32),
@@ -534,16 +732,27 @@
             pltpu.VMEM((REPS, PLANE_ROWS, HD), bf16),
             pltpu.VMEM((REPS, PLANE_ROWS, HD), bf16),
             pltpu.VMEM((2, CACHE + NEW, HD), bf16),
+            pltpu.VMEM((PLANES, WORK, HD), jnp.float32),
+            pltpu.VMEM((PLANES, WORK, HD), jnp.float32),
+            pltpu.VMEM((PLANES, WORK, HD), jnp.float32),
+            pltpu.VMEM((HEADS, NEW, HD), jnp.float32),
+            pltpu.VMEM((HEADS, NEW, HD), jnp.float32),
+            pltpu.VMEM((HEADS, NEW, HD), jnp.float32),
             dma((2,)),
             dma((2,)),
-            dma((3,)),
-            dma((3,)),
+            dma((2,)),
+            dma((W_PIECES,)),
+            dma((W_PIECES,)),
+            dma((W_PIECES,)),
+            dma((W_PIECES,)),
+            dma((W_PIECES,)),
+            dma((W_PIECES,)),
             dma((7,)),
             dma((7,)),
             dma((7,)),
             dma((7,)),
-            dma((16,)),
-            dma((16,)),
+            dma((PLANES,)),
+            dma((PLANES,)),
             dma((1,)),
             dma((1,)),
             dma((PLANES,)),
@@ -570,7 +779,7 @@
         w_kv,
         queries.reshape(NEW, q_cols),
         new_kv.reshape(NEW, HD),
-        lengths,
+        lengths.transpose(0, 2, 1),
         pairing,
         assign.reshape(1, ROWS),
         cache_len.reshape(1, ROWS),

time: 132 us -> 148 us (1.12)
  Pallas kernels: 126 us -> 143 us
    pallas_call x1, Pallas kernels: 126 us -> 143 us  [per_device(): pl.pallas_call(kernel, out_shape=(jax.ShapeDtypeStruct((CACHE, q_cols), b...]
    unnamed x3 -> x2, local copies, waits for them, and re-layouts: 5.3 us -> 3.93 us
where the time goes in v2:
time: 148 us; the launch traced here: 147 us
  Pallas kernels  143 us (97%)
  local copies, waits for them, and re-layouts  3.93 us (3%)
    pallas_call x1, Pallas kernels, per_device(): pl.pallas_call(kernel, out_shape=(jax.ShapeDtypeStruct((CACHE, q_cols), b...  143 us
    unnamed x2, local copies, waits for them, and re-layouts  3.93 us

profile of v2, /device:TPU:1, one launch (start us, length us, event | category | flops | bytes accessed | tf_op | source)
XLA Modules:
  0.0 147.1 jit_solution(6752790615725050798)
XLA Ops:
  0.6 142.5 %shard_map.113 = (bf16[1024,512]{1,0:T(8,128)(2,1)}, bf16[256,512]{1,0:T(8,128)(2,1)}) custom-call(bf16[64,8192]{1,0:T(8,128)(2,1)} %bitcast.10, bf16[8192,512]{1,0:T(8,128)(2,1)} %wq_hbm.1, bf16[8192,128]{1,0:T(8,128)(2,1)} %wkv_hbm.1, bf16[256,512]{1,0:T(8,128)(2,1)} %bitcast.11, bf16[256,128]{1,0:T(8,128)(2,1)} %bitcast.12, s32[2,4,8]{2,1,0:T(4,128)} %bitcast.13, ...), custom_call_target="tpu_custom_call" | custom-call | flops 15032385536 | bytes 11534336 | tf_op jit(solution)/shard_map/pallas_call | solution.py:712
  143.2 2.3 %copy.14 = bf16[1,1,1024,512]{3,2,1,0:T(8,128)(2,1)} copy(bf16[1,1,1024,512]{3,2,1,0:T(8,128)(2,1)} %bitcast.8) | data formatting | bytes 2097152
  145.4 1.7 %copy.15 = bf16[1,1,4,64,512]{4,3,2,1,0:T(8,128)(2,1)} copy(bf16[1,1,4,64,512]{4,3,2,1,0:T(8,128)(2,1)} %bitcast.9) | data formatting | bytes 524288

commit v3 on v1

v3 whole, which is shorter than its diff:
```python
import functools
import math

import jax
import jax.numpy as jnp
import numpy as np
from jax import lax
from jax.experimental import pallas as pl
from jax.experimental.pallas import tpu as pltpu
from jax.sharding import PartitionSpec as P

HD = 128
PLANES = 8
REPS = 8
HEADS = 4
TOK = 64
HALF = 32
PLANE_ROWS = 2 * TOK
WINDOW = 5
STEPS = 4
ROWS = 64
NEW = STEPS * ROWS
CACHE = PLANES * PLANE_ROWS
W_LOW = 2560
K_CHUNK = 2048

theta_base = 500000.0
neg_large = -1e30
exp_scale = math.log2(math.e) / math.sqrt(HD)


def remote(src, dst, send_sem, recv_sem, device):
    pltpu.make_async_remote_copy(
        src_ref=src,
        dst_ref=dst,
        send_sem=send_sem,
        recv_sem=recv_sem,
        device_id=device,
        device_id_type=pl.DeviceIdType.MESH,
    ).start()


def landed(ref, sem):
    pltpu.make_async_copy(ref, ref, sem).wait()


def softmax_mix(scores, values):
    peak = jnp.max(scores, axis=-1, keepdims=True)
    weights = jnp.exp2((scores - peak) * exp_scale)
    total = jnp.sum(weights, axis=-1, keepdims=True)
    mixed = jnp.dot(weights.astype(jnp.bfloat16), values, preferred_element_type=jnp.float32)
    return mixed / total


def starts_of(rows, lens):
    end = jnp.int32(0)
    total = jnp.zeros_like(rows)
    for length in lens:
        end = end + length
        total = total + jnp.where(rows >= end, length, 0)
    return total


def scores_of(query, keys):
    return lax.dot_general(
        query, keys, (((1,), (1,)), ((), ())), preferred_element_type=jnp.float32
    )


def kernel(
    x_hbm,
    wq_hbm,
    wkv_hbm,
    new_ref,
    lengths_ref,
    pairing_ref,
    freq_ref,
    q_out,
    kv_out,
    dec_out,
    xg,
    wq,
    wkv,
    acc,
    cos_t,
    sin_t,
    qhome,
    qstage,
    kvhome,
    kvstage,
    p1,
    p2,
    dec,
    x0_sem,
    xs_send,
    w_sem,
    w_send,
    up_send,
    up_recv,
    down_send,
    down_recv,
    sib_send,
    sib_recv,
    new_send,
    new_recv,
    q_send,
    q_recv,
    kv_send,
    kv_send2,
    kv_recv,
    p1_send,
    p1_recv,
    p2_send,
    p2_recv,
    out_sem,
):
    core = lax.axis_index("pool")
    rep = lax.axis_index("rep")
    t = lax.axis_index("tp")
    z = t // 2
    y = t % 2
    diag = core == y
    off = core != y
    other = 1 - core

    def dev(c2, g2, z2, y2):
        return (c2, g2, z2 * 2 + y2)

    up_dev = dev(core, rep, (z + 1) % PLANES, y)
    down_dev = dev(core, rep, (z + PLANES - 1) % PLANES, y)
    sibling = dev(other, rep, z, y)
    swap_low = dev(other, rep, z, 1 - y)
    swap_high = dev(other, (rep + REPS // 2) % REPS, z, 1 - y)
    across = dev(core, rep, z, 1 - y)
    row0 = pl.multiple_of(core * TOK, TOK)
    other_row0 = pl.multiple_of(other * TOK, TOK)

    wq_low = wq.at[pl.ds(0, W_LOW)]
    wq_high = wq.at[pl.ds(W_LOW, wq.shape[0] - W_LOW)]
    wq_hbm_low = wq_hbm.at[pl.ds(0, W_LOW)]
    wq_hbm_high = wq_hbm.at[pl.ds(W_LOW, wq.shape[0] - W_LOW)]

    def block(slot, half):
        return xg.at[slot, pl.ds(pl.multiple_of(row0 + half * HALF, HALF), HALF)]

    def sibling_block(slot, half):
        return xg.at[slot, pl.ds(pl.multiple_of(other_row0 + half * HALF, HALF), HALF)]

    @pl.when(diag)
    def _():
        for h in range(2):
            pltpu.make_async_copy(
                x_hbm.at[pl.ds(h * HALF, HALF)], block(0, h), x0_sem.at[h]
            ).start()
        pltpu.make_async_copy(wq_hbm_low, wq_low, w_sem.at[0]).start()
        pltpu.make_async_copy(wq_hbm_high, wq_high, w_sem.at[1]).start()
        pltpu.make_async_copy(wkv_hbm, wkv, w_sem.at[2]).start()

    barrier = pltpu.get_barrier_semaphore()

    def greet(n, carry):
        c2 = n // 16
        g2 = (n // 2) % 8
        y2 = n % 2
        mine = (c2 == core) & (g2 == rep) & (y2 == y)

        @pl.when(jnp.logical_not(mine))
        def _():
            pl.semaphore_signal(
                barrier, inc=1, device_id=dev(c2, g2, z, y2), device_id_type=pl.DeviceIdType.MESH
            )

        return carry

    lax.fori_loop(0, 32, greet, 0)
    for device in (up_dev, down_dev):
        pl.semaphore_signal(
            barrier, inc=1, device_id=device, device_id_type=pl.DeviceIdType.MESH
        )
    pl.semaphore_wait(barrier, 33)

    @pl.when(off)
    def _():
        for h in range(2):
            remote(
                x_hbm.at[pl.ds(h * HALF, HALF)],
                sibling_block(0, h),
                xs_send.at[h],
                x0_sem.at[h],
                swap_low,
            )
        remote(wq_hbm_high, wq_high, w_send.at[1], w_sem.at[1], swap_high)
        remote(wq_hbm_low, wq_low, w_send.at[0], w_sem.at[0], swap_low)
        remote(wkv_hbm, wkv, w_send.at[2], w_sem.at[2], swap_low)

    def send_up(src, dst, h, k):
        remote(block(src, h), block(dst, h), up_send.at[k], up_recv.at[k], up_dev)

    def send_down(src, dst, h, k):
        remote(block(src, h), block(dst, h), down_send.at[k], down_recv.at[k], down_dev)

    def share(slot, h):
        k = slot * 2 + h
        remote(block(slot, h), block(slot, h), sib_send.at[k], sib_recv.at[k], sibling)

    for h in range(2):
        landed(block(0, h), x0_sem.at[h])
        send_up(0, 1, h, h)
        send_down(0, 2, h, h)
        share(0, h)

    new_cols = pl.ds(CACHE, NEW)
    remote(new_ref, dec.at[y, new_cols], new_send.at[0], new_recv.at[0], across)
    dec[y, new_cols] = new_ref[...]

    work_lens = [lengths_ref[y, j, rep] for j in range(4)]

    def tables(plane, carry):
        rows = plane * PLANE_ROWS + lax.broadcasted_iota(jnp.int32, (PLANE_ROWS, HD), 0)
        lanes = lax.broadcasted_iota(jnp.int32, (PLANE_ROWS, HD), 1)
        offset = (rows - starts_of(rows, work_lens)).astype(jnp.float32)
        angle = offset * freq_ref[...]
        cos_t[plane] = jnp.cos(angle)
        sine = jnp.sin(angle)
        sin_t[plane] = jnp.where(lanes < HD // 2, -sine, sine)
        return carry

    lax.fori_loop(0, PLANES, tables, 0)

    def relay(d, h):
        k = 2 * (d - 1) + h
        low, high = 2 * d - 1, 2 * d
        landed(block(low, h), up_recv.at[k])
        if d < 3:
            send_up(low, low + 2, h, k + 2)
        elif h == 0:
            send_up(low, low + 2, h, 6)
        share(low, h)
        landed(block(high, h), down_recv.at[k])
        if d < 3:
            send_down(high, high + 2, h, k + 2)
        elif h == 1:
            send_down(high, 7, h, 6)
        share(high, h)

    for d in (1, 2):
        for h in range(2):
            relay(d, h)
    relay(3, 0)
    relay(3, 1)
    landed(wq_low, w_sem.at[0])
    landed(wq_high, w_sem.at[1])
    landed(wkv, w_sem.at[2])

    def finish_plane(slot, plane, rows):
        cosine = cos_t[plane]
        sine = sin_t[plane]

        def turned(part):
            return part * cosine + pltpu.roll(part, HD // 2, 1) * sine

        heads = [turned(rows[:, h * HD : (h + 1) * HD]).astype(jnp.bfloat16) for h in range(HEADS)]
        raw = rows[:, HEADS * HD :]
        own = jnp.where(core == 0, turned(raw), raw).astype(jnp.bfloat16)
        kvstage[plane] = own

        @pl.when(diag)
        def _():
            for h in range(HEADS):
                qhome[plane, h] = heads[h]
            kvhome[core, plane] = own
            remote(
                kvstage.at[plane],
                kvhome.at[core, plane],
                kv_send.at[slot],
                kv_recv.at[core * PLANES + plane],
                across,
            )

        @pl.when(off)
        def _():
            for h in range(HEADS):
                qstage[slot, h] = heads[h]
            remote(
                kvstage.at[plane],
                kvhome.at[core, plane],
                kv_send.at[slot],
                kv_recv.at[core * PLANES + plane],
                swap_low,
            )
            remote(
                kvstage.at[plane],
                kvhome.at[core, plane],
                kv_send2.at[slot],
                kv_recv.at[core * PLANES + plane],
                sibling,
            )
            remote(qstage.at[slot], qhome.at[plane], q_send.at[slot], q_recv.at[plane], swap_low)

        @pl.when(plane == rep)
        def _():
            p1[rep] = own

        @pl.when(plane != rep)
        def _():
            remote(
                kvstage.at[plane],
                p1.at[rep],
                p1_send.at[slot],
                p1_recv.at[rep],
                dev(core, plane, z, y),
            )

    def project(b, carry):
        @pl.when(b == 3)
        def _():
            landed(block(7, 0), up_recv.at[6])
            share(7, 0)
            landed(block(7, 1), down_recv.at[6])
            share(7, 1)

        for j in range(2):
            for h in range(2):
                landed(sibling_block(2 * b + j, h), sib_recv.at[4 * b + 2 * j + h])

        acc[...] = jnp.zeros_like(acc)

        def step(k, inner):
            deep = pl.ds(pl.multiple_of(k * K_CHUNK, K_CHUNK), K_CHUNK)
            rows = xg[pl.ds(2 * b, 2), :, deep].reshape(2 * PLANE_ROWS, K_CHUNK)
            acc[:, : HEADS * HD] += jnp.dot(
                rows, wq[deep, :], preferred_element_type=jnp.float32
            )
            acc[:, HEADS * HD :] += jnp.dot(
                rows, wkv[deep, :], preferred_element_type=jnp.float32
            )
            return inner

        lax.fori_loop(0, wq.shape[0] // K_CHUNK, step, 0)
        finish_plane(2 * b, (z + b) % PLANES, acc[pl.ds(0, PLANE_ROWS), :])
        finish_plane(
            2 * b + 1, (z + 2 * PLANES - 1 - b) % PLANES, acc[pl.ds(PLANE_ROWS, PLANE_ROWS), :]
        )
        return carry

    lax.fori_loop(0, PLANES // 2, project, 0)

    for g2 in range(REPS):

        @pl.when(rep != g2)
        def _():
            landed(p1.at[g2], p1_recv.at[g2])

    cache_rows = pl.ds(pl.multiple_of(rep * PLANE_ROWS, PLANE_ROWS), PLANE_ROWS)

    def hand_over(d, carry):
        p2[d] = p1[pairing_ref[1 - y, d]]
        for y2 in range(2):
            mine = (1 - y == core) & (d == rep) & (y == y2)

            @pl.when(mine)
            def _():
                dec[core, cache_rows] = p2[d]

            @pl.when(jnp.logical_not(mine))
            def _():
                remote(
                    p2.at[d],
                    dec.at[core, cache_rows],
                    p2_send.at[2 * d + y2],
                    p2_recv.at[core * PLANES + rep],
                    dev(1 - y, d, z, y2),
                )

        return carry

    lax.fori_loop(0, REPS, hand_over, 0)

    for plane in range(PLANES):

        @pl.when(off)
        def _():
            landed(qhome.at[plane], q_recv.at[plane])
            landed(kvhome.at[0, plane], kv_recv.at[plane])
            landed(kvhome.at[1, plane], kv_recv.at[PLANES + plane])

        @pl.when(diag)
        def _():
            landed(kvhome.at[other, plane], kv_recv.at[other * PLANES + plane])

    landed(dec.at[1 - y, new_cols], new_recv.at[0])
    for kind in range(2):
        for i in range(REPS):
            mine = (kind == core) & (i == rep) & (off)

            @pl.when(jnp.logical_not(mine))
            def _():
                landed(
                    dec.at[kind, pl.ds(i * PLANE_ROWS, PLANE_ROWS)], p2_recv.at[kind * PLANES + i]
                )

    for source, target, n in ((qhome, q_out, 0), (kvhome, kv_out, 1), (dec, dec_out, 2)):
        pltpu.make_async_copy(source, target, out_sem.at[n]).start()

    landed(new_ref, new_send.at[0])
    for k in range(7):
        landed(block(0, 0), up_send.at[k])
        landed(block(0, 0), down_send.at[k])
    for k in range(16):
        landed(block(0, 0), sib_send.at[k])
    for slot in range(PLANES):
        landed(kvstage.at[0], kv_send.at[slot])

    @pl.when(off)
    def _():
        for h in range(2):
            landed(block(0, h), xs_send.at[h])
        landed(wq_low, w_send.at[0])
        landed(wq_high, w_send.at[1])
        landed(wkv, w_send.at[2])
        for slot in range(PLANES):
            landed(kvstage.at[0], kv_send2.at[slot])
            landed(qstage.at[0], q_send.at[slot])

    def drain(slot, carry):
        high = (z + slot // 2) % PLANES
        low = (z + 2 * PLANES - 1 - slot // 2) % PLANES
        plane = jnp.where(slot % 2 == 0, high, low)

        @pl.when(plane != rep)
        def _():
            landed(kvstage.at[0], p1_send.at[slot])

        for y2 in range(2):
            mine = (1 - y == core) & (slot == rep) & (y == y2)

            @pl.when(jnp.logical_not(mine))
            def _():
                landed(p2.at[0], p2_send.at[2 * slot + y2])

        return carry

    lax.fori_loop(0, PLANES, drain, 0)
    for source, target, n in ((qhome, q_out, 0), (kvhome, kv_out, 1), (dec, dec_out, 2)):
        pltpu.make_async_copy(source, target, out_sem.at[n]).wait()


def attention(
    q_ref,
    kv_ref,
    dec_ref,
    queries_ref,
    lengths_ref,
    pairing_ref,
    assign_ref,
    cache_len_ref,
    prefill_ref,
    decode_ref,
    bias,
):
    core = lax.axis_index("pool")
    rep = lax.axis_index("rep")
    other = 1 - core
    new_cols = pl.ds(CACHE, NEW)
    home_lens = [lengths_ref[core, j, rep] for j in range(4)]
    paired = pairing_ref[core, rep]
    pair_lens = [lengths_ref[other, j, paired] for j in range(4)]

    def column(ref):
        spread = jnp.broadcast_to(ref[...], (ROWS, ROWS))
        here = lax.broadcasted_iota(jnp.int32, (ROWS, ROWS), 0) == lax.broadcasted_iota(
            jnp.int32, (ROWS, ROWS), 1
        )
        picked = jnp.where(here, spread.astype(jnp.float32), 0.0)
        return jnp.sum(picked, axis=1, keepdims=True).astype(jnp.int32)

    member = column(assign_ref)
    limit = column(cache_len_ref)
    lower = jnp.zeros_like(member)
    extent = jnp.zeros_like(member)
    begin = jnp.int32(0)
    for j in range(4):
        lower = jnp.where(member == j, begin, lower)
        extent = jnp.where(member == j, pair_lens[j], extent)
        begin = begin + pair_lens[j]
    upper = lower + jnp.minimum(extent, limit)
    spots = lax.broadcasted_iota(jnp.int32, (ROWS, CACHE), 1)
    visible = jnp.where((spots >= lower) & (spots < upper), 0.0, neg_large)
    new_spot = lax.broadcasted_iota(jnp.int32, (ROWS, NEW), 1)
    row = lax.broadcasted_iota(jnp.int32, (ROWS, NEW), 0)
    for s in range(STEPS):
        rows_here = pl.ds(s * ROWS, ROWS)
        bias[rows_here, pl.ds(0, CACHE)] = visible
        own = (new_spot % ROWS == row) & (new_spot // ROWS <= s)
        bias[rows_here, new_cols] = jnp.where(own, 0.0, neg_large)

    def prefill(i, carry):
        first = jnp.maximum(i - (WINDOW - 1), 0)
        width = WINDOW * PLANE_ROWS
        keys = kv_ref[0, pl.ds(first, WINDOW)].reshape(width, HD)
        values = kv_ref[1, pl.ds(first, WINDOW)].reshape(width, HD)
        row_of = i * PLANE_ROWS + lax.broadcasted_iota(jnp.int32, (PLANE_ROWS, width), 0)
        spot = first * PLANE_ROWS + lax.broadcasted_iota(jnp.int32, (PLANE_ROWS, width), 1)
        begin_of = starts_of(row_of, home_lens)
        mask = jnp.where((spot >= begin_of) & (spot <= row_of), 0.0, neg_large)
        query = q_ref[i].reshape(HEADS * PLANE_ROWS, HD)
        scores = scores_of(query, keys).reshape(HEADS, PLANE_ROWS, width) + mask[None]
        out = softmax_mix(scores.reshape(HEADS * PLANE_ROWS, width), values)
        rows_here = pl.ds(pl.multiple_of(i * PLANE_ROWS, PLANE_ROWS), PLANE_ROWS)
        for h in range(HEADS):
            prefill_ref[rows_here, h * HD : (h + 1) * HD] = out[
                h * PLANE_ROWS : (h + 1) * PLANE_ROWS
            ].astype(jnp.bfloat16)
        return carry

    lax.fori_loop(0, PLANES, prefill, 0)

    for h in range(HEADS):
        scores = scores_of(queries_ref[:, h * HD : (h + 1) * HD], dec_ref[0]) + bias[...]
        decode_ref[:, h * HD : (h + 1) * HD] = softmax_mix(scores, dec_ref[1]).astype(jnp.bfloat16)


def per_device(prompt_states, w_query, w_kv, queries, new_kv, lengths, pairing, assign, cache_len):
    depth = prompt_states.shape[-1]
    q_cols = w_query.shape[1]
    half = np.arange(HD // 2, dtype=np.float32) / np.float32(HD // 2)
    inverse = np.power(np.float32(theta_base), -half).astype(np.float32)
    freq = jnp.asarray(np.concatenate([inverse, inverse])[None, :])
    vmem = pl.BlockSpec(memory_space=pltpu.VMEM)
    smem = pl.BlockSpec(memory_space=pltpu.SMEM)
    anywhere = pl.BlockSpec(memory_space=pl.ANY)
    dma = pltpu.SemaphoreType.DMA
    bf16 = jnp.bfloat16
    lengths_here = lengths.transpose(0, 2, 1)
    q_home, kv_home, caches = pl.pallas_call(
        kernel,
        out_shape=(
            jax.ShapeDtypeStruct((PLANES, HEADS, PLANE_ROWS, HD), bf16),
            jax.ShapeDtypeStruct((2, PLANES, PLANE_ROWS, HD), bf16),
            jax.ShapeDtypeStruct((2, CACHE + NEW, HD), bf16),
        ),
        in_specs=[anywhere, anywhere, anywhere, vmem, smem, smem, vmem],
        out_specs=(anywhere, anywhere, anywhere),
        scratch_shapes=[
            pltpu.VMEM((PLANES, PLANE_ROWS, depth), bf16),
            pltpu.VMEM((depth, q_cols), bf16),
            pltpu.VMEM((depth, HD), bf16),
            pltpu.VMEM((2 * PLANE_ROWS, q_cols + HD), jnp.float32),
            pltpu.VMEM((PLANES, PLANE_ROWS, HD), jnp.float32),
            pltpu.VMEM((PLANES, PLANE_ROWS, HD), jnp.float32),
            pltpu.VMEM((PLANES, HEADS, PLANE_ROWS, HD), bf16),
            pltpu.VMEM((PLANES, HEADS, PLANE_ROWS, HD), bf16),
            pltpu.VMEM((2, PLANES, PLANE_ROWS, HD), bf16),
            pltpu.VMEM((PLANES, PLANE_ROWS, HD), bf16),
            pltpu.VMEM((REPS, PLANE_ROWS, HD), bf16),
            pltpu.VMEM((REPS, PLANE_ROWS, HD), bf16),
            pltpu.VMEM((2, CACHE + NEW, HD), bf16),
            dma((2,)),
            dma((2,)),
            dma((3,)),
            dma((3,)),
            dma((7,)),
            dma((7,)),
            dma((7,)),
            dma((7,)),
            dma((16,)),
            dma((16,)),
            dma((1,)),
            dma((1,)),
            dma((PLANES,)),
            dma((PLANES,)),
            dma((PLANES,)),
            dma((PLANES,)),
            dma((2 * PLANES,)),
            dma((PLANES,)),
            dma((REPS,)),
            dma((2 * REPS,)),
            dma((2 * REPS,)),
            dma((3,)),
        ],
        compiler_params=pltpu.CompilerParams(
            collective_id=0, has_side_effects=True, vmem_limit_bytes=56 * 1024 * 1024
        ),
        cost_estimate=pl.CostEstimate(
            flops=2 * CACHE * depth * (q_cols + HD),
            bytes_accessed=2 * depth * (q_cols + HD + TOK),
            transcendentals=2 * CACHE * HD,
        ),
    )(
        prompt_states.reshape(TOK, depth),
        w_query,
        w_kv,
        new_kv.reshape(NEW, HD),
        lengths_here,
        pairing,
        freq,
    )
    prefill_out, decode_out = pl.pallas_call(
        attention,
        out_shape=(
            jax.ShapeDtypeStruct((CACHE, q_cols), bf16),
            jax.ShapeDtypeStruct((NEW, q_cols), bf16),
        ),
        in_specs=[vmem, vmem, vmem, vmem, smem, smem, vmem, vmem],
        out_specs=(vmem, vmem),
        scratch_shapes=[pltpu.VMEM((NEW, CACHE + NEW), jnp.float32)],
        compiler_params=pltpu.CompilerParams(vmem_limit_bytes=32 * 1024 * 1024),
        cost_estimate=pl.CostEstimate(
            flops=8 * CACHE * CACHE * q_cols,
            bytes_accessed=8 * CACHE * q_cols,
            transcendentals=2 * HEADS * CACHE * CACHE,
        ),
    )(
        q_home,
        kv_home,
        caches,
        queries.reshape(NEW, q_cols),
        lengths_here,
        pairing,
        assign.reshape(1, ROWS),
        cache_len.reshape(1, ROWS),
    )
    return (
        prefill_out.reshape(1, 1, CACHE, q_cols),
        decode_out.reshape(1, 1, STEPS, ROWS, q_cols),
    )


def solution(mesh):
    placed = (
        P("pool", "rep", "tp", None),
        P(None, "tp"),
        P(None, "tp"),
        P("pool", "rep", None, None, "tp"),
        P("pool", "rep", None, None, "tp"),
        P(),
        P(),
        P("pool", "rep", None),
        P("pool", "rep", None),
    )
    return jax.shard_map(
        per_device,
        mesh=mesh,
        in_specs=placed,
        out_specs=(P("pool", "rep", None, "tp"), P("pool", "rep", None, None, "tp")),
        check_vma=False,
    )
```

time: 132 us -> 143 us (1.083); the launches traced: 132 us -> 141 us
  Pallas kernels: 126 us -> 137 us
  local copies, waits for them, and re-layouts: 5.3 us -> 3.37 us
    pallas_call x1 -> x2, Pallas kernels: 126 us -> 137 us  [the longest x1 125 us: per_device(): pl.pallas_call(kernel, out_shape=(jax.ShapeDtypeStruct((PLANES, HEADS, PL...]
    unnamed x3 -> x16, local copies, waits for them, and re-layouts: 5.3 us -> 3.37 us
where the time goes in v3:
time: 143 us; the launch traced here: 141 us
  Pallas kernels  137 us (96%)
  local copies, waits for them, and re-layouts  3.37 us (2%)
    pallas_call x1, Pallas kernels, per_device(): pl.pallas_call(kernel, out_shape=(jax.ShapeDtypeStruct((PLANES, HEADS, PL...  125 us
    pallas_call x1, Pallas kernels, per_device(): pl.pallas_call(attention, out_shape=(jax.ShapeDtypeStruct((CACHE, q_cols)...  12 us
    unnamed x16, local copies, waits for them, and re-layouts  3.37 us

profile of v3, /device:TPU:1, one launch (start us, length us, event | category | flops | bytes accessed | tf_op | source)
XLA Modules:
  0.0 140.8 jit_solution(18166607589727888908)
XLA Ops:
  0.6 0.0 copy-start
  0.6 0.0 copy-start.1
  0.7 0.0 copy-start.2
  0.7 0.0 copy-start.3
  0.7 0.0 copy-start.4
  0.7 124.7 %shard_map.113 = (bf16[8,4,128,128]{3,2,1,0:T(8,128)(2,1)}, bf16[2,8,128,128]{3,2,1,0:T(8,128)(2,1)}, bf16[2,1280,128]{2,1,0:T(8,128)(2,1)}) custom-call(bf16[64,8192]{1,0:T(8,128)(2,1)} %bitcast.13, bf16[8192,512]{1,0:T(8,128)(2,1)} %wq_hbm.1, bf16[8192,128]{1,0:T(8,128)(2,1)} %wkv_hbm.1, bf16[256,128]{1,0:T(8,128)(2,1)} %bitcast.14, s32[2,4,8]{2,1,0:T(4,128)} %bitcast.9, ...), custom_call_target="tpu_custom_call" | custom-call | flops 10737418240 | bytes 11534336 | tf_op jit(solution)/shard_map/pallas_call | solution.py:535
  125.4 0.0 copy-done
  125.4 0.0 copy-done.1
  125.5 0.0 copy-done.2
  125.5 0.0 copy-done.3
  125.5 0.0 copy-done.4
  125.5 0.0 copy-start.5
  125.5 1.2 copy-done.5
  126.7 0.0 copy-start.6
  126.7 1.1 copy-done.6
  127.8 0.0 copy-start.7
  127.8 1.0 copy-done.7
  128.8 12.0 %shard_map.114 = (bf16[1024,512]{1,0:T(8,128)(2,1)}, bf16[256,512]{1,0:T(8,128)(2,1)}) custom-call(bf16[8,4,128,128]{3,2,1,0:T(8,128)(2,1)S(1)} %copy-done.5, bf16[2,8,128,128]{3,2,1,0:T(8,128)(2,1)S(1)} %copy-done.7, bf16[2,1280,128]{2,1,0:T(8,128)(2,1)S(1)} %copy-done.6, bf16[256,512]{1,0:T(8,128)(2,1)S(1)} %bitcast.8, s32[2,4,8]{2,1,0:T(4,128)S(1)} %bitcast.10, ...), custom_call_target="tpu_custom_call" | custom-call | flops 4294967296 | bytes 4194304 | tf_op jit(solution)/shard_map/pallas_call | solution.py:598
Async XLA Ops:
  0.6 124.8 %copy-start = (bf16[1,1,4,64,512]{4,3,2,1,0:T(8,128)(2,1)S(1)}, bf16[1,1,4,64,512]{4,3,2,1,0:T(8,128)(2,1)}, u32[]{:S(2)}) copy-start(bf16[1,1,4,64,512]{4,3,2,1,0:T(8,128)(2,1)} %param.13) | copy-start | bytes 786436
  0.6 124.8 %copy-start.1 = (s32[2,8,4]{1,2,0:T(4,128)S(1)}, s32[2,8,4]{1,2,0:T(4,128)}, u32[]{:S(2)}) copy-start(s32[2,8,4]{1,2,0:T(4,128)} %param.15) | copy-start | bytes 772
  0.7 124.8 %copy-start.2 = (s32[2,8]{1,0:T(2,128)S(1)}, s32[2,8]{1,0:T(2,128)}, u32[]{:S(2)}) copy-start(s32[2,8]{1,0:T(2,128)} %pairing_ref.3) | copy-start | bytes 196
  0.7 124.8 %copy-start.3 = (s32[1,1,64]{2,1,0:T(1,128)S(1)}, s32[1,1,64]{2,1,0:T(1,128)}, u32[]{:S(2)}) copy-start(s32[1,1,64]{2,1,0:T(1,128)} %param.17) | copy-start | bytes 772
  0.7 124.8 %copy-start.4 = (s32[1,1,64]{2,1,0:T(1,128)S(1)}, s32[1,1,64]{2,1,0:T(1,128)}, u32[]{:S(2)}) copy-start(s32[1,1,64]{2,1,0:T(1,128)} %param.18) | copy-start | bytes 772
  125.5 1.2 copy-start.5
  126.7 1.1 copy-start.6
  127.8 1.0 copy-start.7

commit v4 on v2

--- a/solution.py
+++ b/solution.py
@@ -23,7 +23,7 @@
 W_PIECE = 256
 W_LOW_PIECES = 3
 W_PIECES = 8
-N_TILE = 256
+K_CHUNK = 2048
 WORK = HEADS * PLANE_ROWS
 
 theta_base = 500000.0
@@ -62,7 +62,8 @@
     pairing_ref,
     assign_ref,
     cache_len_ref,
-    freq_ref,
+    cos_hbm,
+    sin_hbm,
     prefill_ref,
     decode_ref,
     xg,
@@ -85,6 +86,7 @@
     dec_top,
     dec_total,
     dec_mix,
+    tab_sem,
     x0_sem,
     xs_send,
     wl_sem,
@@ -180,6 +182,9 @@
         wkv_hbm.at[pl.ds(own_depth, depth)], wall.at[:, near_kv_cols], wl_sem.at[1]
     ).start()
 
+    pltpu.make_async_copy(cos_hbm, cos_t, tab_sem.at[0]).start()
+    pltpu.make_async_copy(sin_hbm, sin_t, tab_sem.at[1]).start()
+
     barrier = pltpu.get_barrier_semaphore()
 
     def greet(n, carry):
@@ -284,14 +289,30 @@
     paired = pairing_ref[core, rep]
     pair_lens = [lengths_ref[other, j, paired] for j in range(4)]
 
+    work_starts = [jnp.int32(0)]
+    for j in range(3):
+        work_starts.append(work_starts[j] + work_lens[j])
+    landed(cos_t, tab_sem.at[0])
+    landed(sin_t, tab_sem.at[1])
+
+    def table_row(ref, row):
+        return ref[row // PLANE_ROWS, pl.ds(row % PLANE_ROWS, 1), :]
+
+    start_cos = [table_row(cos_t, row) for row in work_starts]
+    start_sin = [table_row(sin_t, row) for row in work_starts]
+
     def tables(plane, carry):
         rows = plane * PLANE_ROWS + lax.broadcasted_iota(jnp.int32, (PLANE_ROWS, HD), 0)
-        lanes = lax.broadcasted_iota(jnp.int32, (PLANE_ROWS, HD), 1)
-        offset = (rows - starts_of(rows, work_lens)).astype(jnp.float32)
-        angle = offset * freq_ref[...]
-        cos_t[plane] = jnp.cos(angle)
-        sine = jnp.sin(angle)
-        sin_t[plane] = jnp.where(lanes < HD // 2, -sine, sine)
+        cos_b = jnp.broadcast_to(start_cos[0], (PLANE_ROWS, HD))
+        sin_b = jnp.broadcast_to(start_sin[0], (PLANE_ROWS, HD))
+        for j in range(1, 4):
+            later = rows >= work_starts[j]
+            cos_b = jnp.where(later, start_cos[j], cos_b)
+            sin_b = jnp.where(later, start_sin[j], sin_b)
+        cos_a = cos_t[plane]
+        sin_a = sin_t[plane]
+        cos_t[plane] = cos_a * cos_b + sin_a * sin_b
+        sin_t[plane] = sin_a * cos_b - cos_a * sin_b
         return carry
 
     lax.fori_loop(0, PLANES, tables, 0)
@@ -400,14 +421,16 @@
     def project(first, count):
         rows_here = count * PLANE_ROWS
 
-        def tile(n, carry):
-            wide = pl.ds(pl.multiple_of(n * N_TILE, N_TILE), N_TILE)
-            rows = xg[pl.ds(first, count)].reshape(rows_here, depth)
-            out = jnp.dot(rows, wall[:, wide], preferred_element_type=jnp.float32)
-            accs[pl.ds(first, count), :, wide] = out.reshape(count, PLANE_ROWS, N_TILE)
+        accs[pl.ds(first, count)] = jnp.zeros((count, PLANE_ROWS, wall.shape[1]), jnp.float32)
+
+        def step(k, carry):
+            deep = pl.ds(pl.multiple_of(k * K_CHUNK, K_CHUNK), K_CHUNK)
+            rows = xg[pl.ds(first, count), :, deep].reshape(rows_here, K_CHUNK)
+            out = jnp.dot(rows, wall[deep, :], preferred_element_type=jnp.float32)
+            accs[pl.ds(first, count)] += out.reshape(count, PLANE_ROWS, wall.shape[1])
             return carry
 
-        lax.fori_loop(0, wall.shape[1] // N_TILE, tile, 0)
+        lax.fori_loop(0, depth // K_CHUNK, step, 0)
         for slot in range(first, first + count):
             remote(
                 accs.at[slot, :, sibling_cols],
@@ -635,9 +658,6 @@
     attend_near()
     relay(3, 1)
     project(5, 2)
-    landed(dec.at[1 - y, new_cols], new_recv.at[0])
-    caches_landed(near)
-    decode_first(near)
     finish(((5, -3), (6, 3)))
     hand_over(3, 3)
     for away in (-3, 3):
@@ -649,6 +669,9 @@
     project(7, 1)
     finish(((7, 4),))
     hand_over(4, 4)
+    landed(dec.at[1 - y, new_cols], new_recv.at[0])
+    caches_landed(near)
+    decode_first(near)
     home_landed(4)
     attend_last()
     settle(True)
@@ -698,12 +721,21 @@
     lax.fori_loop(0, PLANES, drain, 0)
 
 
+def hand_out(prefill_in, decode_in, prefill_ref, decode_ref):
+    prefill_ref[...] = prefill_in[...]
+    decode_ref[...] = decode_in[...]
+
+
 def per_device(prompt_states, w_query, w_kv, queries, new_kv, lengths, pairing, assign, cache_len):
     depth = prompt_states.shape[-1]
     q_cols = w_query.shape[1]
-    half = np.arange(HD // 2, dtype=np.float32) / np.float32(HD // 2)
-    inverse = np.power(np.float32(theta_base), -half).astype(np.float32)
-    freq = jnp.asarray(np.concatenate([inverse, inverse])[None, :])
+    powers = np.arange(HD // 2, dtype=np.float32) / np.float32(HD // 2)
+    inverse = np.power(np.float32(theta_base), -powers).astype(np.float64)
+    angle = np.arange(CACHE, dtype=np.float64)[:, None] * inverse[None, :]
+    cosine, sine = np.cos(angle), np.sin(angle)
+    table_shape = (PLANES, PLANE_ROWS, HD)
+    cos_table = np.concatenate([cosine, cosine], axis=1).astype(np.float32).reshape(table_shape)
+    sin_table = np.concatenate([-sine, sine], axis=1).astype(np.float32).reshape(table_shape)
     vmem = pl.BlockSpec(memory_space=pltpu.VMEM)
     smem = pl.BlockSpec(memory_space=pltpu.SMEM)
     anywhere = pl.BlockSpec(memory_space=pl.ANY)
@@ -715,7 +747,7 @@
             jax.ShapeDtypeStruct((CACHE, q_cols), bf16),
             jax.ShapeDtypeStruct((NEW, q_cols), bf16),
         ),
-        in_specs=[anywhere, anywhere, anywhere, vmem, vmem, smem, smem, vmem, vmem, vmem],
+        in_specs=[anywhere, anywhere, anywhere, vmem, vmem, smem, smem, vmem, vmem, anywhere, anywhere],
         out_specs=(vmem, vmem),
         scratch_shapes=[
             pltpu.VMEM((PLANES, PLANE_ROWS, depth // 2), bf16),
@@ -738,6 +770,7 @@
             pltpu.VMEM((HEADS, NEW, HD), jnp.float32),
             pltpu.VMEM((HEADS, NEW, HD), jnp.float32),
             pltpu.VMEM((HEADS, NEW, HD), jnp.float32),
+            dma((2,)),
             dma((2,)),
             dma((2,)),
             dma((2,)),
@@ -783,8 +816,19 @@
         pairing,
         assign.reshape(1, ROWS),
         cache_len.reshape(1, ROWS),
-        freq,
+        jnp.asarray(cos_table),
+        jnp.asarray(sin_table),
     )
+    prefill_out, decode_out = pl.pallas_call(
+        hand_out,
+        out_shape=(
+            jax.ShapeDtypeStruct((CACHE, q_cols), bf16),
+            jax.ShapeDtypeStruct((NEW, q_cols), bf16),
+        ),
+        in_specs=[vmem, vmem],
+        out_specs=(vmem, vmem),
+        compiler_params=pltpu.CompilerParams(vmem_limit_bytes=62 * 1024 * 1024),
+    )(prefill_out, decode_out)
     return (
         prefill_out.reshape(1, 1, CACHE, q_cols),
         decode_out.reshape(1, 1, STEPS, ROWS, q_cols),

time: 148 us -> 144 us (0.973)
  local copies, waits for them, and re-layouts: 3.93 us -> 0 us
    unnamed x2 -> x0, local copies, waits for them, and re-layouts: 3.93 us -> none
    pallas_call x1, Pallas kernels: 143 us -> 139 us  [per_device(): pl.pallas_call(kernel, out_shape=(jax.ShapeDtypeStruct((CACHE, q_cols), b...]
    pallas_call x0 -> x1, Pallas kernels: none -> 2.38 us  [per_device(): pl.pallas_call(hand_out, out_shape=(jax.ShapeDtypeStruct((CACHE, q_cols),...]
where the time goes in v4:
time: 144 us; the launch traced here: 142 us
  Pallas kernels  142 us (99%)
    pallas_call x1, Pallas kernels, per_device(): pl.pallas_call(kernel, out_shape=(jax.ShapeDtypeStruct((CACHE, q_cols), b...  139 us

profile of v4, /device:TPU:1, one launch (start us, length us, event | category | flops | bytes accessed | tf_op | source)
XLA Modules:
  0.0 142.4 jit_solution(16250546227914003975)
XLA Ops:
  0.6 139.4 %shard_map.122 = (bf16[1024,512]{1,0:T(8,128)(2,1)}, bf16[256,512]{1,0:T(8,128)(2,1)}) custom-call(bf16[64,8192]{1,0:T(8,128)(2,1)} %bitcast.8, bf16[8192,512]{1,0:T(8,128)(2,1)} %wq_hbm.1, bf16[8192,128]{1,0:T(8,128)(2,1)} %wkv_hbm.1, bf16[256,512]{1,0:T(8,128)(2,1)} %bitcast.10, bf16[256,128]{1,0:T(8,128)(2,1)} %bitcast.12, s32[2,4,8]{2,1,0:T(4,128)} %bitcast.13, ...), custom_call_target="tpu_custom_call" | custom-call | flops 15032385536 | bytes 11534336 | tf_op jit(solution)/shard_map/pallas_call | solution.py:744
  140.0 2.4 %shard_map.123 = (bf16[1024,512]{1,0:T(8,128)(2,1)}, bf16[256,512]{1,0:T(8,128)(2,1)}) custom-call(bf16[1024,512]{1,0:T(8,128)(2,1)} %get-tuple-element.6.prefill_in, bf16[256,512]{1,0:T(8,128)(2,1)} %get-tuple-element.7.decode_in), custom_call_target="tpu_custom_call" | custom-call | tf_op jit(solution)/shard_map/pallas_call | solution.py:822
